TPU v7x, 512 devices: a whole 4x8x8 slice. The times are simulated.
512 devices in a mesh: blk: 64 (over z, y_hi, x), col: 8 (over y_lo, core).
Axes of the slice: x: 4, y: 8 (y_hi: 2, y_lo: 4; y = y_hi * 4 + y_lo), z: 8, core: 2. Of those that a mesh axis runs over, the one named last changes fastest.
Arguments:
- queries: bfloat16 [512, 16384], P('blk', 'col'), may hold values from -6 to 6
- factor: bfloat16 [16384, 1024], P('col', 'blk'), may hold values from -0.046875 to 0.046875
- eigenvalues: float32 [1024], replicated, may hold values from 0.05 to 20
- damping: float32 [1], replicated, may hold values from 0.5 to 2
- train_rows: bfloat16 [65536, 16384], P('blk', 'col'), may hold values from -0.046875 to 0.046875
Outputs:
- scores: bfloat16 [512, 65536], P('col', 'blk')
All inputs are finite; a program needn't handle non-finite values.
Results may differ from a plain program's by a relative error of at most 0.0049.
Values may be sent and summed in bfloat16 or wider, within the bound.
No kernel may reach another device: no remote copies, remote signals or barrier semaphores. Data moves between devices by JAX's collectives and lax.ppermute only.
A program may use at most 64 MiB of HBM per device.

v0:
```python
import jax
import jax.numpy as jnp
from jax import lax
from jax.sharding import Mesh
from jax.sharding import PartitionSpec as P

BLK = ("blk_0", "blk_1", "blk_2")


def in_order(tiles, dim):
    shape = list(tiles.shape[1:])
    shape[dim] *= tiles.shape[0]
    return jnp.moveaxis(tiles, 0, dim).reshape(shape)


def stacked_from(shard, axes, turns):
    tiles = shard[None]
    for k in turns:
        tiles = lax.all_gather(tiles, axes[k], axis=0, tiled=True)
    carried = [lax.axis_size(axes[k]) for k in reversed(turns)]
    tiles = tiles.reshape(*carried, *shard.shape)
    turned = sorted(range(len(turns)), key=lambda place: turns[len(turns) - 1 - place])
    return tiles.transpose(*turned, *range(len(turns), tiles.ndim)).reshape(-1, *shard.shape)


def gather_axes(shard, axes, turns, dim):
    return in_order(stacked_from(shard, axes, turns), dim)


def from_everyone(shard, axis):
    length = lax.axis_size(axis)
    return lax.all_to_all(
        jnp.broadcast_to(shard[None], (length, *shard.shape)), axis, 0, 0, tiled=True
    )


def taken_together(shard, axis):
    return from_everyone(shard, axis).sum(axis=0)


def row_scores(block_rows, train_rows):
    return jnp.einsum("qk,nk->qn", block_rows, train_rows, preferred_element_type=jnp.float32)


def per_device(queries, factor, eigenvalues, damping, train_rows):
    damp_value = damping[0]
    weights = eigenvalues / (eigenvalues + damp_value)
    full_factor = gather_axes(factor, BLK, (1, 0, 2), 1)
    partial_value = jnp.dot(queries, full_factor, preferred_element_type=jnp.float32)
    coefficient = taken_together(partial_value, "col")
    scaled = coefficient * weights[None, :]
    correction = jnp.dot(scaled, full_factor.astype(jnp.float32).T, precision=lax.Precision.HIGHEST)
    pre_own = ((queries.astype(jnp.float32) - correction) / damp_value).astype(jnp.bfloat16)
    partial_scores = row_scores(lax.all_gather(pre_own, BLK, axis=0, tiled=True), train_rows)
    scores = lax.psum_scatter(partial_scores, "col", scatter_dimension=0, tiled=True)
    return scores.astype(jnp.bfloat16)


def solution(mesh):
    split = Mesh(
        mesh.devices.reshape(8, 2, 4, mesh.shape["col"]), ("blk_0", "blk_1", "blk_2", "col")
    )
    in_specs = (P(BLK, "col"), P("col", BLK), P(), P(), P(BLK, "col"))
    out_specs = P("col", BLK)
    return jax.shard_map(
        per_device, mesh=split, in_specs=in_specs, out_specs=out_specs, check_vma=False
    )
```

profile of v0, /device:TPU:6, one launch (start us, length us, event | category | flops | bytes accessed | tf_op | source)
XLA Modules:
  0.0 330.9 jit_solution(12432319824471753628)
XLA Ops:
  6.5 0.0 all-gather.5.cloned.1.call-start
  6.5 9.7 %all-gather = bf16[4096,16]{0,1:T(8,128)(2,1)S(1)} all-gather(bf16[2048,16]{0,1:T(8,128)(2,1)} %param.6), channel_id=2, replica_groups=mesh['blk_0'=8,'blk_1'=2,'blk_2'=4,'col'=8] {'blk_1'}, dimensions={0}, use_global_device_ids=true | all-gather | bytes 196608 | tf_op jit(solution)/shard_map/all_gather | solution.py:19
  16.2 0.7 copy.17
  16.9 0.0 all-gather.5.cloned.1.call-update
  16.9 0.0 all-gather.7.cloned.1.call-start
  17.0 47.4 %all-gather.5.cloned.1.call-done = bf16[16,2048,16]{1,2,0:T(8,128)(2,1)} async-done(((bf16[2,2048,16]{1,2,0:T(8,128)(2,1)}), bf16[16,2048,16]{1,2,0:T(8,128)(2,1)}) %all-gather.5.cloned.1.call-update) | async-done | bytes 1048592 | tf_op jit(solution)/shard_map/all_gather | solution.py:19
  64.4 0.0 all-gather.7.cloned.1.call-update
  64.4 52.0 %all-gather.7.cloned.1.call-done = bf16[64,2048,16]{1,2,0:T(8,128)(2,1)} async-done(((bf16[16,2048,16]{1,2,0:T(8,128)(2,1)}), bf16[64,2048,16]{1,2,0:T(8,128)(2,1)}) %all-gather.7.cloned.1.call-update) | async-done | bytes 4194320 | tf_op jit(solution)/shard_map/all_gather | solution.py:19
  116.4 0.0 copy-start.1
  116.4 2.5 copy.14
  118.9 0.0 copy-start
  118.9 0.0 copy-start.2
  118.9 1.9 copy-done
  120.9 0.0 copy-done.1
  120.9 1.2 fusion.4
  122.1 0.7 broadcast_in_dim.5
  122.8 4.8 %all-to-all-start = ((f32[8,8,1024]{2,1,0:T(8,128)}), f32[8,8,1024]{2,1,0:T(8,128)S(1)}, u32[]{:S(2)}, u32[]{:S(2)}) async-start(f32[8,8,1024]{2,1,0:T(8,128)} %broadcast_in_dim.5), calls=%async_computation | async-start | bytes 524288 | tf_op jit(solution)/shard_map/all_to_all | solution.py:32
  127.6 0.0 all-gather.9.cloned.1.call-start
  128.3 0.0 copy-done.2
  128.4 9.0 %all-to-all-done = f32[8,8,1024]{2,1,0:T(8,128)S(1)} async-done(((f32[8,8,1024]{2,1,0:T(8,128)}), f32[8,8,1024]{2,1,0:T(8,128)S(1)}, u32[]{:S(2)}, u32[]{:S(2)}) %all-to-all-start) | async-done | bytes 262176 | tf_op jit(solution)/shard_map/all_to_all | solution.py:32
  137.4 4.5 %fusion.1 = bf16[8,2048]{1,0:T(8,128)(2,1)} fusion(bf16[2048,1024]{0,1:T(8,128)(2,1)} %bitcast.21, bf16[8,2048]{1,0:T(8,128)(2,1)S(1)} %copy-done.1, f32[]{:T(128)} %bitcast.19, f32[8,1024]{1,0:T(8,128)S(1)} %reduce_sum.9, f32[1024]{0:T(1024)S(1)} %add_divide_fusion), kind=kOutput, calls=%fused_computation.2 | convolution fusion | flops 201400320 | bytes 4296708 | tf_op jit(solution)/shard_map/dot_general | solution.py:52
  142.0 0.0 all-gather.9.cloned.1.call-update
  142.0 0.0 reduce-scatter.2.cloned.1.call-start
  142.0 134.0 %all-gather.9.cloned.1.call-done = bf16[512,2048]{1,0:T(8,128)(2,1)} async-done(((bf16[8,2048]{1,0:T(8,128)(2,1)}), bf16[512,2048]{1,0:T(8,128)(2,1)}) %all-gather.9.cloned.1.call-update) | async-done | bytes 2097168 | tf_op jit(solution)/shard_map/all_gather | solution.py:54
  276.1 6.5 %fusion.5 = f32[512,1024]{1,0:T(8,128)} fusion(bf16[512,2048]{1,0:T(8,128)(2,1)} %all-gather.9.cloned.1.call-done, bf16[1024,2048]{1,0:T(8,128)(2,1)} %param.9), kind=kOutput, calls=%fused_computation.8 | convolution fusion | flops 2147483648 | bytes 8388608 | tf_op jit(solution)/shard_map/qk,nk->qn/dot_general | solution.py:42
  282.6 0.0 reduce-scatter.2.cloned.1.call-update
  282.6 40.1 %reduce-scatter.2.cloned.1.call-done = f32[64,1024]{1,0:T(8,128)} async-done(((f32[512,1024]{1,0:T(8,128)}), f32[64,1024]{1,0:T(8,128)}) %reduce-scatter.2.cloned.1.call-update) | async-done | bytes 262160 | tf_op jit(solution)/shard_map/reduce_scatter | solution.py:55
  322.7 1.6 convert_element_type.12
  (2 shorter events, 0.0 us)
Async XLA Ops:
  6.5 57.8 %all-gather.5.cloned.1.call-start = ((), (), s32[]{:S(2)}) async-start(), calls=%async_computation.2 | async-start | bytes 1179648 | tf_op jit(solution)/shard_map/all_gather | solution.py:19
  16.9 99.5 %all-gather.7.cloned.1.call-start = ((), (), s32[]{:S(2)}) async-start(), calls=%async_computation.3 | async-start | bytes 5242880 | tf_op jit(solution)/shard_map/all_gather | solution.py:19
  116.4 4.5 %copy-start.1 = (bf16[8,2048]{1,0:T(8,128)(2,1)S(1)}, bf16[8,2048]{1,0:T(8,128)(2,1)}, u32[]{:S(2)}) copy-start(bf16[8,2048]{1,0:T(8,128)(2,1)} %param.5) | copy-start | bytes 98308
  118.9 2.0 copy-start
  118.9 9.4 %copy-start.2 = (f32[1024]{0:T(1024)S(1)}, f32[1024]{0:T(1024)}, u32[]{:S(2)}) copy-start(f32[1024]{0:T(1024)} %param.7) | copy-start | bytes 12292
  122.8 14.6 %all-to-all-start = ((f32[8,8,1024]{2,1,0:T(8,128)}), f32[8,8,1024]{2,1,0:T(8,128)S(1)}, u32[]{:S(2)}, u32[]{:S(2)}) async-start(f32[8,8,1024]{2,1,0:T(8,128)} %broadcast_in_dim.5), calls=%async_computation | async-start | bytes 524288 | tf_op jit(solution)/shard_map/all_to_all | solution.py:32
  127.6 148.4 %all-gather.9.cloned.1.call-start = ((), (), s32[]{:S(2)}) async-start(), calls=%async_computation.4 | async-start | bytes 2129920 | tf_op jit(solution)/shard_map/all_gather | solution.py:54
  142.0 180.7 %reduce-scatter.2.cloned.1.call-start = ((), (), s32[]{:S(2)}) async-start(), calls=%async_computation.5 | async-start | bytes 2359296 | tf_op jit(solution)/shard_map/reduce_scatter | solution.py:55
Sparse Core Ops, SparseCore 0:
  17.1 47.2 all-gather.4
  66.5 49.8 all-gather.6
  142.1 133.9 all-gather.8
  282.7 39.9 reduce-scatter.1
where the time goes:
time: 331 us
  waiting for transfers between devices  283 us (85%)
  between operations  13.8 us (4%)
  matrix products  12.2 us (4%)
  blocking collectives  9.7 us (3%)
  local copies, waits for them, and re-layouts  5.85 us (2%)
  starting transfers between devices  4.97 us (2%)
    all_gather x1, waiting for transfers between devices, per_device(): lax.all_gather(pre_own, BLK, axis=0, tiled=True)  134 us
    all_gather x2, waiting for transfers between devices, stacked_from(): tiles = lax.all_gather(tiles, axes[k], axis=0, tiled=True)  99.4 us
    reduce_scatter x1, waiting for transfers between devices, per_device(): lax.psum_scatter(partial_scores, 'col', scatter_dimension=0, tiled=True)  40.1 us
    all_gather x1, blocking collectives, stacked_from(): tiles = lax.all_gather(tiles, axes[k], axis=0, tiled=True)  9.7 us
    all_to_all x1, waiting for transfers between devices, from_everyone(): lax.all_to_all(jnp.broadcast_to(shard[None], (length, *shard.shape)), axi...  9.03 us
  transfers between devices with their start and end apart: 5, of which 5 were waited for; matrix products, arithmetic and copies ran while one was open for 0% of the time, Pallas kernels for 0%

commit v1 on v0

v1 whole, which is shorter than its diff:
```python
import jax
import jax.numpy as jnp
from jax import lax
from jax.sharding import Mesh
from jax.sharding import PartitionSpec as P

BLK = ("z", "yh", "x")
COL = ("yl", "core")
ROWS = ("z", "yh")


def exchanged(tiles, axes):
    return lax.all_to_all(tiles, axes, 0, 0, tiled=True)


def everyones(shard, axes):
    size = lax.axis_size(axes)
    tiles = exchanged(jnp.broadcast_to(shard[None], (size, *shard.shape)), axes)
    return tiles.reshape(size * shard.shape[0], *shard.shape[1:])


def nt(left, right):
    return lax.dot_general(
        left, right, (((1,), (1,)), ((), ())), preferred_element_type=jnp.float32
    )


def per_device(queries, factor, eigenvalues, damping, train_rows):
    rows, width = queries.shape
    ranks = factor.shape[1]
    cores, n_yl, n_x = lax.axis_size("core"), lax.axis_size("yl"), lax.axis_size("x")
    n_rows = lax.axis_size(ROWS)
    damp_value = damping[0]

    by_x = everyones(queries, "x")
    basis = everyones(factor.T, ROWS)

    mine = lax.dynamic_index_in_dim(
        eigenvalues.reshape(n_rows, n_x, ranks), lax.axis_index("x"), 1, keepdims=False
    ).reshape(-1)
    weights = mine / (mine + damp_value)

    partial_value = nt(by_x, basis)
    size = lax.axis_size(COL)
    coefficient = exchanged(
        jnp.broadcast_to(partial_value[None], (size, *partial_value.shape)), COL
    ).sum(axis=0)
    scaled = coefficient * weights[None, :]
    high = scaled.astype(jnp.bfloat16)
    low = (scaled - high.astype(jnp.float32)).astype(jnp.bfloat16)
    partial_correction = jnp.dot(high, basis, preferred_element_type=jnp.float32) + jnp.dot(
        low, basis, preferred_element_type=jnp.float32
    )
    terms = exchanged(
        partial_correction.astype(jnp.bfloat16).reshape(n_x, rows, width), "x"
    )
    correction = terms.astype(jnp.float32).sum(axis=0)
    pre_own = ((queries.astype(jnp.float32) - correction) / damp_value).astype(jnp.bfloat16)

    pre_rows = everyones(pre_own, ROWS)
    pre = everyones(pre_rows, "x")
    partial_scores = nt(pre, train_rows).reshape(n_x, n_yl, cores, -1, train_rows.shape[0])
    core = lax.axis_index("core")
    kept = lax.dynamic_index_in_dim(partial_scores, core, 2, keepdims=False)
    sent = lax.dynamic_index_in_dim(partial_scores, 1 - core, 2, keepdims=False)
    came = lax.ppermute(sent.astype(jnp.bfloat16), "core", [(0, 1), (1, 0)])
    pair = (kept + came.astype(jnp.float32)).astype(jnp.bfloat16)
    parts = exchanged(pair.transpose(1, 0, 2, 3), "yl")
    scores = parts.astype(jnp.float32).sum(axis=0)
    n_yh = lax.axis_size("yh")
    scores = scores.reshape(n_x, n_yh, rows, -1).transpose(1, 0, 2, 3)
    return scores.astype(jnp.bfloat16).reshape(n_x * n_yh * rows, -1)


def solution(mesh):
    split = Mesh(mesh.devices.reshape(8, 2, 4, 4, 2), BLK + COL)
    in_specs = (P(BLK, COL), P(COL, BLK), P(), P(), P(BLK, COL))
    out_specs = P(COL, BLK)
    return jax.shard_map(
        per_device, mesh=split, in_specs=in_specs, out_specs=out_specs, check_vma=False
    )
```

time: 331 us -> 165 us (0.50)
  the two profiles are of different devices: /device:TPU:6 before, /device:TPU:56 now
where the time goes in v1:
time: 165 us
  blocking collectives  103 us (62%)
  waiting for transfers between devices  33.4 us (20%)
  starting transfers between devices  13.9 us (8%)
  local copies, waits for them, and re-layouts  6.43 us (4%)
  matrix products  5.54 us (3%)
    all_to_all x5, blocking collectives, exchanged(): return lax.all_to_all(tiles, axes, 0, 0, tiled=True)  103 us
    all_to_all x2, waiting for transfers between devices, exchanged(): return lax.all_to_all(tiles, axes, 0, 0, tiled=True)  31.5 us
    all_to_all x2, starting transfers between devices, exchanged(): return lax.all_to_all(tiles, axes, 0, 0, tiled=True)  12 us
    dot_general x2, matrix products, nt(): lax.dot_general(left, right, (((1,), (1,)), ((), ())), preferred_element_...  4.95 us
    broadcast_in_dim x4, local copies, waits for them, and re-layouts, everyones(): tiles = exchanged(jnp.broadcast_to(shard[None], (size, *shard.shape)), axes)  3.37 us
  transfers between devices with their start and end apart: 3, of which 3 were waited for; matrix products, arithmetic and copies ran while one was open for 0% of the time, Pallas kernels for 0%

profile of v1, /device:TPU:56, one launch (start us, length us, event | category | flops | bytes accessed | tf_op | source)
XLA Modules:
  0.0 164.6 jit_solution(13377978251520887018)
XLA Ops:
  0.0 0.8 broadcast_in_dim.12
  0.8 10.1 %all_to_all.35 = bf16[4,8,2048]{2,1,0:T(8,128)(2,1)S(1)} all-to-all(bf16[4,8,2048]{2,1,0:T(8,128)(2,1)S(1)} %broadcast_in_dim.12), channel_id=1, replica_groups=mesh['z'=8,'yh'=2,'x'=4,'yl'=4,'core'=2] {'x'}, dimensions={0} | all-to-all | bytes 262144 | tf_op jit(solution)/shard_map/all_to_all | solution.py:13
  10.8 0.9 broadcast_in_dim.13
  11.8 0.0 copy-start.2
  11.8 43.4 %all_to_all.36 = bf16[16,16,2048]{2,1,0:T(8,128)(2,1)S(1)} all-to-all(bf16[16,16,2048]{2,1,0:T(8,128)(2,1)S(1)} %broadcast_in_dim.13), channel_id=1, replica_groups=mesh['z'=8,'yh'=2,'x'=4,'yl'=4,'core'=2] {'z','yh'}, dimensions={0} | all-to-all | bytes 2097152 | tf_op jit(solution)/shard_map/all_to_all | solution.py:13
  55.2 0.4 fusion.7
  55.6 0.7 broadcast_in_dim.14
  56.3 0.0 copy-start.1
  56.3 8.4 %all-to-all-start.2 = ((f32[8,32,256]{2,1,0:T(8,128)}), f32[8,32,256]{2,1,0:T(8,128)S(1)}, u32[]{:S(2)}, u32[]{:S(2)}) async-start(f32[8,32,256]{2,1,0:T(8,128)} %broadcast_in_dim.14), calls=%async_computation.2 | async-start | bytes 524288 | tf_op jit(solution)/shard_map/all_to_all | solution.py:13
  64.7 0.0 copy-done.2
  64.7 0.1 reshape.42
  64.8 0.1 reshape.43
  65.6 6.3 %all-to-all-done.2 = f32[8,32,256]{2,1,0:T(8,128)S(1)} async-done(((f32[8,32,256]{2,1,0:T(8,128)}), f32[8,32,256]{2,1,0:T(8,128)S(1)}, u32[]{:S(2)}, u32[]{:S(2)}) %all-to-all-start.2) | async-done | bytes 262176 | tf_op jit(solution)/shard_map/all_to_all | solution.py:13
  71.9 0.3 fusion.9
  72.2 0.3 fusion.3
  72.5 8.4 %all_to_all.37 = bf16[4,8,2048]{2,1,0:T(8,128)(2,1)S(1)} all-to-all(bf16[4,8,2048]{2,1,0:T(8,128)(2,1)S(1)} %fusion.3), channel_id=1, replica_groups=mesh['z'=8,'yh'=2,'x'=4,'yl'=4,'core'=2] {'x'}, dimensions={0} | all-to-all | bytes 262144 | tf_op jit(solution)/shard_map/all_to_all | solution.py:13
  80.9 0.0 copy-done.1
  81.0 23.9 %all_to_all.38 = bf16[16,8,2048]{2,1,0:T(8,128)(2,1)S(1)} all-to-all(bf16[16,8,2048]{2,1,0:T(8,128)(2,1)S(1)} %broadcast_in_dim.15), channel_id=1, replica_groups=mesh['z'=8,'yh'=2,'x'=4,'yl'=4,'core'=2] {'z','yh'}, dimensions={0} | all-to-all | bytes 1048576 | tf_op jit(solution)/shard_map/all_to_all | solution.py:13
  104.9 1.6 broadcast_in_dim.17
  106.5 3.6 %all-to-all-start.5 = ((bf16[4,128,2048]{2,1,0:T(8,128)(2,1)}), bf16[4,128,2048]{2,1,0:T(8,128)(2,1)S(1)}, u32[]{:S(2)}, u32[]{:S(2)}) async-start(bf16[4,128,2048]{2,1,0:T(8,128)(2,1)} %broadcast_in_dim.17), calls=%async_computation.5 | async-start | bytes 4194304 | tf_op jit(solution)/shard_map/all_to_all | solution.py:13
  110.1 25.2 %all-to-all-done.5 = bf16[4,128,2048]{2,1,0:T(8,128)(2,1)S(1)} async-done(((bf16[4,128,2048]{2,1,0:T(8,128)(2,1)}), bf16[4,128,2048]{2,1,0:T(8,128)(2,1)S(1)}, u32[]{:S(2)}, u32[]{:S(2)}) %all-to-all-start.5) | async-done | bytes 2097184 | tf_op jit(solution)/shard_map/all_to_all | solution.py:13
  135.3 4.5 %fusion = f32[4,4,2,16,1024]{4,3,2,1,0:T(8,128)S(1)} fusion(bf16[4,4,2,16,2048]{4,3,2,1,0:T(8,128)(2,1)S(1)} %bitcast.39, bf16[1024,2048]{1,0:T(8,128)(2,1)} %param.9), kind=kOutput, calls=%fused_computation | convolution fusion | flops 2147483648 | bytes 8388608 | tf_op jit(solution)/shard_map/dot_general | solution.py:23
  139.9 0.0 copy-start
  139.9 1.3 copy-done
  141.2 0.1 fusion.5
  141.3 1.9 %collective-permute-start = (bf16[4,4,16,1024]{3,2,1,0:T(8,128)(2,1)S(1)}, bf16[4,4,16,1024]{3,2,1,0:T(8,128)(2,1)S(1)}, u32[]{:S(2)}, u32[]{:S(2)}) collective-permute-start(bf16[4,4,16,1024]{3,2,1,0:T(8,128)(2,1)S(1)} %fusion.5), channel_id=1, source_target_pairs={{0,1},{1,0},{2,3},{3,2},{4,5},{5,4},{6,7},{7,6},{8,9},{9,8},{10,11... | collective-permute-start | bytes 1572872 | tf_op jit(solution)/shard_map/ppermute | solution.py:66
  143.2 1.9 %collective-permute-done = bf16[4,4,16,1024]{3,2,1,0:T(8,128)(2,1)S(1)} collective-permute-done((bf16[4,4,16,1024]{3,2,1,0:T(8,128)(2,1)S(1)}, bf16[4,4,16,1024]{3,2,1,0:T(8,128)(2,1)S(1)}, u32[]{:S(2)}, u32[]{:S(2)}) %collective-permute-start) | collective-permute-done | bytes 524320 | tf_op jit(solution)/shard_map/ppermute | solution.py:66
  145.1 1.4 fusion.6
  146.5 17.3 %all_to_all.39 = bf16[4,4,16,1024]{3,2,1,0:T(8,128)(2,1)S(1)} all-to-all(bf16[4,4,16,1024]{3,2,1,0:T(8,128)(2,1)S(1)} %copy.9), channel_id=1, replica_groups=mesh['z'=8,'yh'=2,'x'=4,'yl'=4,'core'=2] {'yl'}, dimensions={0} | all-to-all | bytes 1048576 | tf_op jit(solution)/shard_map/all_to_all | solution.py:13
  163.9 0.1 reduce_sum.32
  163.9 0.7 copy.10
  (7 shorter events, 0.2 us)
Async XLA Ops:
  11.8 52.9 %copy-start.2 = (f32[1024]{0:T(1024)S(1)}, f32[1024]{0:T(1024)}, u32[]{:S(2)}) copy-start(f32[1024]{0:T(1024)} %param.7) | copy-start | bytes 12292
  56.3 24.6 %copy-start.1 = (bf16[8,2048]{1,0:T(8,128)(2,1)S(1)}, bf16[8,2048]{1,0:T(8,128)(2,1)}, u32[]{:S(2)}) copy-start(bf16[8,2048]{1,0:T(8,128)(2,1)} %param.5) | copy-start | bytes 98308
  56.3 15.6 %all-to-all-start.2 = ((f32[8,32,256]{2,1,0:T(8,128)}), f32[8,32,256]{2,1,0:T(8,128)S(1)}, u32[]{:S(2)}, u32[]{:S(2)}) async-start(f32[8,32,256]{2,1,0:T(8,128)} %broadcast_in_dim.14), calls=%async_computation.2 | async-start | bytes 524288 | tf_op jit(solution)/shard_map/all_to_all | solution.py:13
  106.5 28.8 %all-to-all-start.5 = ((bf16[4,128,2048]{2,1,0:T(8,128)(2,1)}), bf16[4,128,2048]{2,1,0:T(8,128)(2,1)S(1)}, u32[]{:S(2)}, u32[]{:S(2)}) async-start(bf16[4,128,2048]{2,1,0:T(8,128)(2,1)} %broadcast_in_dim.17), calls=%async_computation.5 | async-start | bytes 4194304 | tf_op jit(solution)/shard_map/all_to_all | solution.py:13
  139.9 1.4 copy-start
  141.3 3.8 %collective-permute-start = (bf16[4,4,16,1024]{3,2,1,0:T(8,128)(2,1)S(1)}, bf16[4,4,16,1024]{3,2,1,0:T(8,128)(2,1)S(1)}, u32[]{:S(2)}, u32[]{:S(2)}) collective-permute-start(bf16[4,4,16,1024]{3,2,1,0:T(8,128)(2,1)S(1)} %fusion.5), channel_id=1, source_target_pairs={{0,1},{1,0},{2,3},{3,2},{4,5},{5,4},{6,7},{7,6},{8,9},{9,8},{10,11... | collective-permute-start | bytes 1572872 | tf_op jit(solution)/shard_map/ppermute | solution.py:66

commit v2 on v1

v2 whole, which is shorter than its diff:
```python
import jax
import jax.numpy as jnp
from jax import lax
from jax.sharding import Mesh
from jax.sharding import PartitionSpec as P

BLK = ("z", "yh", "x")
COL = ("yl", "core")
ROWS = ("z", "yh")
PLANE = ("x", "yh")


def exchanged(tiles, axes):
    return lax.all_to_all(tiles, axes, 0, 0, tiled=True)


def everyones(shard, axes):
    size = lax.axis_size(axes)
    tiles = exchanged(jnp.broadcast_to(shard[None], (size, *shard.shape)), axes)
    return tiles.reshape(size * shard.shape[0], *shard.shape[1:])


def from_next(shard, axis, step):
    size = lax.axis_size(axis)
    return lax.ppermute(shard, axis, [((i + step) % size, i) for i in range(size)])


def nt(left, right):
    return lax.dot_general(
        left, right, (((1,), (1,)), ((), ())), preferred_element_type=jnp.float32
    )


def per_device(queries, factor, eigenvalues, damping, train_rows):
    rows, width = queries.shape
    ranks = factor.shape[1]
    n_x, n_z = lax.axis_size("x"), lax.axis_size("z")
    x, core = lax.axis_index("x"), lax.axis_index("core")
    damp_value = damping[0]

    basis = everyones(factor.T, "z")
    near = everyones(queries, PLANE)

    mine = lax.dynamic_index_in_dim(
        eigenvalues.reshape(n_z, -1, ranks), lax.axis_index(("yh", "x")), 1, keepdims=False
    ).reshape(-1)
    weights = mine / (mine + damp_value)

    partial_value = nt(near, basis).astype(jnp.bfloat16)
    coefficient = everyones(partial_value[None], COL).astype(jnp.float32).sum(axis=0)
    scaled = coefficient * weights[None, :]
    partial_correction = jnp.dot(
        scaled.astype(jnp.bfloat16), basis, preferred_element_type=jnp.float32
    )
    terms = exchanged(
        partial_correction.astype(jnp.bfloat16).reshape(-1, rows, width), PLANE
    )
    correction = terms.astype(jnp.float32).sum(axis=0)
    pre_own = ((queries.astype(jnp.float32) - correction) / damp_value).astype(jnp.bfloat16)

    chunk = everyones(pre_own, ROWS)
    half = chunk.shape[0] // 2
    after = from_next(chunk, "x", 1)
    before = from_next(chunk, "x", n_x - 1)
    far_after = from_next(after[:half], "x", 1)
    far_before = from_next(before[half:], "x", n_x - 1)

    def reduced_on_chip(blocks):
        value = nt(jnp.concatenate(blocks, 0), train_rows)
        value = value.reshape(-1, lax.axis_size("yl"), 2, chunk.shape[0] // n_z, train_rows.shape[0])
        kept = lax.dynamic_index_in_dim(value, core, 2, keepdims=False)
        sent = lax.dynamic_index_in_dim(value, 1 - core, 2, keepdims=False)
        came = lax.ppermute(sent.astype(jnp.bfloat16), "core", [(0, 1), (1, 0)])
        return (kept + came.astype(jnp.float32)).astype(jnp.bfloat16)

    first = reduced_on_chip((chunk, after, before))
    last = reduced_on_chip((far_after, far_before))
    pair = jnp.concatenate([first[:2], last, first[2:]], 0)
    parts = exchanged(pair.transpose(1, 0, 2, 3), "yl")
    scores = parts.astype(jnp.float32).sum(axis=0).astype(jnp.bfloat16)
    scores = lax.dynamic_slice_in_dim(jnp.concatenate([scores, scores], 0), n_x - x, n_x)
    n_yh = lax.axis_size("yh")
    scores = scores.reshape(n_x, n_yh, rows, -1).transpose(1, 0, 2, 3)
    return scores.reshape(n_x * n_yh * rows, -1)


def solution(mesh):
    split = Mesh(mesh.devices.reshape(8, 2, 4, 4, 2), BLK + COL)
    in_specs = (P(BLK, COL), P(COL, BLK), P(), P(), P(BLK, COL))
    out_specs = P(COL, BLK)
    return jax.shard_map(
        per_device, mesh=split, in_specs=in_specs, out_specs=out_specs, check_vma=False
    )
```

time: 165 us -> 155 us (0.939)
  the two profiles are of different devices: /device:TPU:56 before, /device:TPU:6 now
where the time goes in v2:
time: 155 us; the launch traced here: 153 us
  blocking collectives  79.6 us (51%)
  starting transfers between devices  34 us (22%)
  waiting for transfers between devices  28 us (18%)
  matrix products  6.05 us (4%)
  local copies, waits for them, and re-layouts  3.45 us (2%)
    all_to_all x4, blocking collectives, exchanged(): return lax.all_to_all(tiles, axes, 0, 0, tiled=True)  79.6 us
    all_to_all x2, waiting for transfers between devices, exchanged(): return lax.all_to_all(tiles, axes, 0, 0, tiled=True)  20.9 us
    all_to_all x2, starting transfers between devices, exchanged(): return lax.all_to_all(tiles, axes, 0, 0, tiled=True)  15.3 us
    ppermute x4, starting transfers between devices, from_next(): lax.ppermute(shard, axis, [((i + step) % size, i) for i in range(size)])  14.4 us
    ppermute x4, waiting for transfers between devices, from_next(): lax.ppermute(shard, axis, [((i + step) % size, i) for i in range(size)])  6.26 us
    dot_general x3, matrix products, nt(): lax.dot_general(left, right, (((1,), (1,)), ((), ())), preferred_element_...  5.83 us
    ppermute x2, starting transfers between devices, reduced_on_chip(): came = lax.ppermute(sent.astype(jnp.bfloat16), 'core', [(0, 1), (1, 0)])  4.33 us
  transfers between devices with their start and end apart: 8, of which 4 were waited for; matrix products, arithmetic and copies ran while one was open for 4% of the time, Pallas kernels for 0%

profile of v2, /device:TPU:6, one launch (start us, length us, event | category | flops | bytes accessed | tf_op | source)
XLA Modules:
  0.0 153.2 jit_solution(5971364268344145951)
XLA Ops:
  0.0 0.0 copy-start.1
  0.0 0.0 copy-start.2
  0.0 0.8 broadcast_in_dim.8
  0.9 18.7 %all_to_all.30 = bf16[8,8,2048]{2,1,0:T(8,128)(2,1)S(1)} all-to-all(bf16[8,8,2048]{2,1,0:T(8,128)(2,1)S(1)} %broadcast_in_dim.8), channel_id=1, replica_groups=mesh['z'=8,'yh'=2,'x'=4,'yl'=4,'core'=2] {'x','yh'}, dimensions={0} | all-to-all | bytes 524288 | tf_op jit(solution)/shard_map/all_to_all | solution.py:14
  19.6 0.9 broadcast_in_dim.9
  20.5 26.2 %all_to_all.31 = bf16[8,16,2048]{2,1,0:T(8,128)(2,1)S(1)} all-to-all(bf16[8,16,2048]{2,1,0:T(8,128)(2,1)S(1)} %broadcast_in_dim.9), channel_id=1, replica_groups=mesh['z'=8,'yh'=2,'x'=4,'yl'=4,'core'=2] {'z'}, dimensions={0} | all-to-all | bytes 1048576 | tf_op jit(solution)/shard_map/all_to_all | solution.py:14
  46.7 0.3 convolution_convert_fusion.1
  47.0 0.7 broadcast_in_dim.10
  47.7 6.0 %all-to-all-start.2 = ((bf16[8,1,64,128]{3,2,1,0:T(8,128)(2,1)}), bf16[8,1,64,128]{3,2,1,0:T(8,128)(2,1)S(1)}, u32[]{:S(2)}, u32[]{:S(2)}) async-start(bf16[8,1,64,128]{3,2,1,0:T(8,128)(2,1)} %broadcast_in_dim.10), calls=%async_computation.2 | async-start | bytes 262144 | tf_op jit(solution)/shard_map/all_to_all | solution.py:14
  53.7 0.0 copy-done.2
  53.7 0.1 reshape.64
  53.8 0.1 reshape.65
  54.5 5.9 %all-to-all-done.2 = bf16[8,1,64,128]{3,2,1,0:T(8,128)(2,1)S(1)} async-done(((bf16[8,1,64,128]{3,2,1,0:T(8,128)(2,1)}), bf16[8,1,64,128]{3,2,1,0:T(8,128)(2,1)S(1)}, u32[]{:S(2)}, u32[]{:S(2)}) %all-to-all-start.2) | async-done | bytes 131104 | tf_op jit(solution)/shard_map/all_to_all | solution.py:14
  60.5 0.2 fusion
  60.7 13.7 %all_to_all.32 = bf16[8,8,2048]{2,1,0:T(8,128)(2,1)S(1)} all-to-all(bf16[8,8,2048]{2,1,0:T(8,128)(2,1)S(1)} %fusion), channel_id=1, replica_groups=mesh['z'=8,'yh'=2,'x'=4,'yl'=4,'core'=2] {'x','yh'}, dimensions={0} | all-to-all | bytes 524288 | tf_op jit(solution)/shard_map/all_to_all | solution.py:14
  74.4 0.0 copy-done.1
  74.5 21.0 %all_to_all.33 = bf16[16,8,2048]{2,1,0:T(8,128)(2,1)S(1)} all-to-all(bf16[16,8,2048]{2,1,0:T(8,128)(2,1)S(1)} %broadcast_in_dim.11), channel_id=1, replica_groups=mesh['z'=8,'yh'=2,'x'=4,'yl'=4,'core'=2] {'z','yh'}, dimensions={0} | all-to-all | bytes 1048576 | tf_op jit(solution)/shard_map/all_to_all | solution.py:14
  95.5 3.0 %collective-permute-start = (bf16[128,2048]{1,0:T(8,128)(2,1)S(1)}, bf16[128,2048]{1,0:T(8,128)(2,1)S(1)}, u32[]{:S(2)}, u32[]{:S(2)}) collective-permute-start(bf16[128,2048]{1,0:T(8,128)(2,1)S(1)} %bitcast.46), channel_id=1, source_target_pairs={{8,0},{16,8},{24,16},{0,24},{9,1},{17,9},{25,17},{1,25},{10,2},{18... | collective-permute-start | bytes 1572872 | tf_op jit(solution)/shard_map/ppermute | solution.py:25
  98.5 4.0 %collective-permute-start.1 = (bf16[128,2048]{1,0:T(8,128)(2,1)S(1)}, bf16[128,2048]{1,0:T(8,128)(2,1)S(1)}, u32[]{:S(2)}, u32[]{:S(2)}) collective-permute-start(bf16[128,2048]{1,0:T(8,128)(2,1)S(1)} %bitcast.47), channel_id=1, source_target_pairs={{24,0},{0,8},{8,16},{16,24},{25,1},{1,9},{9,17},{17,25},{26,2},{2,... | collective-permute-start | bytes 1572872 | tf_op jit(solution)/shard_map/ppermute | solution.py:25
  102.5 6.3 %collective-permute-done = bf16[128,2048]{1,0:T(8,128)(2,1)S(1)} collective-permute-done((bf16[128,2048]{1,0:T(8,128)(2,1)S(1)}, bf16[128,2048]{1,0:T(8,128)(2,1)S(1)}, u32[]{:S(2)}, u32[]{:S(2)}) %collective-permute-start) | collective-permute-done | bytes 524320 | tf_op jit(solution)/shard_map/ppermute | solution.py:25
  108.8 2.6 %collective-permute-start.3 = (bf16[64,2048]{1,0:T(8,128)(2,1)S(1)}, bf16[64,2048]{1,0:T(8,128)(2,1)S(1)}, u32[]{:S(2)}, u32[]{:S(2)}) collective-permute-start(bf16[64,2048]{1,0:T(8,128)(2,1)S(1)} %slice.17), channel_id=1, source_target_pairs={{8,0},{16,8},{24,16},{0,24},{9,1},{17,9},{25,17},{1,25},{10,2},{18... | collective-permute-start | bytes 786440 | tf_op jit(solution)/shard_map/ppermute | solution.py:25
  111.4 0.0 collective-permute-done.1
  111.5 0.0 copy-start
  111.5 4.7 %collective-permute-start.4 = (bf16[64,2048]{1,0:T(8,128)(2,1)S(1)}, bf16[64,2048]{1,0:T(8,128)(2,1)S(1)}, u32[]{:S(2)}, u32[]{:S(2)}) collective-permute-start(bf16[64,2048]{1,0:T(8,128)(2,1)S(1)} %slice.18), channel_id=1, source_target_pairs={{24,0},{0,8},{8,16},{16,24},{25,1},{1,9},{9,17},{17,25},{26,2},{2,... | collective-permute-start | bytes 786440 | tf_op jit(solution)/shard_map/ppermute | solution.py:25
  116.2 4.0 %fusion.1 = f32[384,1024]{1,0:T(8,128)S(1)} fusion(bf16[1024,2048]{1,0:T(8,128)(2,1)} %param.9, bf16[128,2048]{1,0:T(8,128)(2,1)S(1)} %collective-permute-done.1, bf16[128,2048]{1,0:T(8,128)(2,1)S(1)} %collective-permute-done, bf16[128,2048]{1,0:T(8,128)(2,1)S(1)} %bitcast.48), kind=kOutput, calls=%fused_computation.2 | convolution fusion | flops 1615331328 | bytes 7340032 | tf_op jit(solution)/shard_map/dot_general | solution.py:29
  120.2 0.1 fusion.12
  120.3 1.9 %collective-permute-start.2 = (bf16[3,4,16,1024]{3,2,0,1:T(8,128)(2,1)S(1)}, bf16[3,4,16,1024]{3,2,0,1:T(8,128)(2,1)S(1)}, u32[]{:S(2)}, u32[]{:S(2)}) collective-permute-start(bf16[3,4,16,1024]{3,2,0,1:T(8,128)(2,1)S(1)} %fusion.12), channel_id=1, source_target_pairs={{0,1},{1,0},{2,3},{3,2},{4,5},{5,4},{6,7},{7,6},{8,9},{9,8},{10,11... | collective-permute-start | bytes 1179656 | tf_op jit(solution)/shard_map/ppermute | solution.py:73
  122.2 0.0 collective-permute-done.3
  122.2 0.0 collective-permute-done.4
  122.2 0.0 copy-done
  122.2 1.5 fusion.8
  123.8 2.4 %collective-permute-start.5 = (bf16[1,4,16,1024]{3,2,0,1:T(8,128)(2,1)S(1)}, bf16[1,4,16,1024]{3,2,0,1:T(8,128)(2,1)S(1)}, u32[]{:S(2)}, u32[]{:S(2)}) collective-permute-start(bf16[1,4,16,1024]{3,2,0,1:T(8,128)(2,1)S(1)} %fusion.15), channel_id=1, source_target_pairs={{0,1},{1,0},{2,3},{3,2},{4,5},{5,4},{6,7},{7,6},{8,9},{9,8},{10,11... | collective-permute-start | bytes 393224 | tf_op jit(solution)/shard_map/ppermute | solution.py:73
  126.2 0.0 collective-permute-done.2
  126.2 0.1 fusion.7
  126.4 0.8 collective-permute-done.5
  127.2 0.8 maximum_bitcast_fusion
  128.0 9.3 %all-to-all-start.5 = ((bf16[4,4,16,1024]{3,2,1,0:T(8,128)(2,1)}), bf16[4,4,16,1024]{3,2,1,0:T(8,128)(2,1)S(1)}, u32[]{:S(2)}, u32[]{:S(2)}) async-start(bf16[4,4,16,1024]{3,2,1,0:T(8,128)(2,1)} %maximum_bitcast_fusion), calls=%async_computation.5 | async-start | bytes 1048576 | tf_op jit(solution)/shard_map/all_to_all | solution.py:14
  137.3 15.0 %all-to-all-done.5 = bf16[4,4,16,1024]{3,2,1,0:T(8,128)(2,1)S(1)} async-done(((bf16[4,4,16,1024]{3,2,1,0:T(8,128)(2,1)}), bf16[4,4,16,1024]{3,2,1,0:T(8,128)(2,1)S(1)}, u32[]{:S(2)}, u32[]{:S(2)}) %all-to-all-start.5) | async-done | bytes 524320 | tf_op jit(solution)/shard_map/all_to_all | solution.py:14
  152.3 0.1 reduce_sum.32
  152.4 0.1 fusion.17
  152.5 0.7 copy.17
  (12 shorter events, 0.3 us)
Async XLA Ops:
  0.0 74.4 %copy-start.1 = (bf16[8,2048]{1,0:T(8,128)(2,1)S(1)}, bf16[8,2048]{1,0:T(8,128)(2,1)}, u32[]{:S(2)}) copy-start(bf16[8,2048]{1,0:T(8,128)(2,1)} %param.5) | copy-start | bytes 98308
  0.0 53.7 %copy-start.2 = (f32[1024]{0:T(1024)S(1)}, f32[1024]{0:T(1024)}, u32[]{:S(2)}) copy-start(f32[1024]{0:T(1024)} %param.7) | copy-start | bytes 12292
  47.7 12.8 %all-to-all-start.2 = ((bf16[8,1,64,128]{3,2,1,0:T(8,128)(2,1)}), bf16[8,1,64,128]{3,2,1,0:T(8,128)(2,1)S(1)}, u32[]{:S(2)}, u32[]{:S(2)}) async-start(bf16[8,1,64,128]{3,2,1,0:T(8,128)(2,1)} %broadcast_in_dim.10), calls=%async_computation.2 | async-start | bytes 262144 | tf_op jit(solution)/shard_map/all_to_all | solution.py:14
  95.5 13.3 %collective-permute-start = (bf16[128,2048]{1,0:T(8,128)(2,1)S(1)}, bf16[128,2048]{1,0:T(8,128)(2,1)S(1)}, u32[]{:S(2)}, u32[]{:S(2)}) collective-permute-start(bf16[128,2048]{1,0:T(8,128)(2,1)S(1)} %bitcast.46), channel_id=1, source_target_pairs={{8,0},{16,8},{24,16},{0,24},{9,1},{17,9},{25,17},{1,25},{10,2},{18... | collective-permute-start | bytes 1572872 | tf_op jit(solution)/shard_map/ppermute | solution.py:25
  98.5 13.0 %collective-permute-start.1 = (bf16[128,2048]{1,0:T(8,128)(2,1)S(1)}, bf16[128,2048]{1,0:T(8,128)(2,1)S(1)}, u32[]{:S(2)}, u32[]{:S(2)}) collective-permute-start(bf16[128,2048]{1,0:T(8,128)(2,1)S(1)} %bitcast.47), channel_id=1, source_target_pairs={{24,0},{0,8},{8,16},{16,24},{25,1},{1,9},{9,17},{17,25},{26,2},{2,... | collective-permute-start | bytes 1572872 | tf_op jit(solution)/shard_map/ppermute | solution.py:25
  108.8 13.4 %collective-permute-start.3 = (bf16[64,2048]{1,0:T(8,128)(2,1)S(1)}, bf16[64,2048]{1,0:T(8,128)(2,1)S(1)}, u32[]{:S(2)}, u32[]{:S(2)}) collective-permute-start(bf16[64,2048]{1,0:T(8,128)(2,1)S(1)} %slice.17), channel_id=1, source_target_pairs={{8,0},{16,8},{24,16},{0,24},{9,1},{17,9},{25,17},{1,25},{10,2},{18... | collective-permute-start | bytes 786440 | tf_op jit(solution)/shard_map/ppermute | solution.py:25
  111.5 10.8 %copy-start = (bf16[1024,2048]{1,0:T(8,128)(2,1)S(1)}, bf16[1024,2048]{1,0:T(8,128)(2,1)}, u32[]{:S(2)}) copy-start(bf16[1024,2048]{1,0:T(8,128)(2,1)} %param.9) | copy-start | bytes 12582916
  111.5 10.7 %collective-permute-start.4 = (bf16[64,2048]{1,0:T(8,128)(2,1)S(1)}, bf16[64,2048]{1,0:T(8,128)(2,1)S(1)}, u32[]{:S(2)}, u32[]{:S(2)}) collective-permute-start(bf16[64,2048]{1,0:T(8,128)(2,1)S(1)} %slice.18), channel_id=1, source_target_pairs={{24,0},{0,8},{8,16},{16,24},{25,1},{1,9},{9,17},{17,25},{26,2},{2,... | collective-permute-start | bytes 786440 | tf_op jit(solution)/shard_map/ppermute | solution.py:25
  120.3 5.9 %collective-permute-start.2 = (bf16[3,4,16,1024]{3,2,0,1:T(8,128)(2,1)S(1)}, bf16[3,4,16,1024]{3,2,0,1:T(8,128)(2,1)S(1)}, u32[]{:S(2)}, u32[]{:S(2)}) collective-permute-start(bf16[3,4,16,1024]{3,2,0,1:T(8,128)(2,1)S(1)} %fusion.12), channel_id=1, source_target_pairs={{0,1},{1,0},{2,3},{3,2},{4,5},{5,4},{6,7},{7,6},{8,9},{9,8},{10,11... | collective-permute-start | bytes 1179656 | tf_op jit(solution)/shard_map/ppermute | solution.py:73
  123.8 3.4 %collective-permute-start.5 = (bf16[1,4,16,1024]{3,2,0,1:T(8,128)(2,1)S(1)}, bf16[1,4,16,1024]{3,2,0,1:T(8,128)(2,1)S(1)}, u32[]{:S(2)}, u32[]{:S(2)}) collective-permute-start(bf16[1,4,16,1024]{3,2,0,1:T(8,128)(2,1)S(1)} %fusion.15), channel_id=1, source_target_pairs={{0,1},{1,0},{2,3},{3,2},{4,5},{5,4},{6,7},{7,6},{8,9},{9,8},{10,11... | collective-permute-start | bytes 393224 | tf_op jit(solution)/shard_map/ppermute | solution.py:73
  128.0 24.3 %all-to-all-start.5 = ((bf16[4,4,16,1024]{3,2,1,0:T(8,128)(2,1)}), bf16[4,4,16,1024]{3,2,1,0:T(8,128)(2,1)S(1)}, u32[]{:S(2)}, u32[]{:S(2)}) async-start(bf16[4,4,16,1024]{3,2,1,0:T(8,128)(2,1)} %maximum_bitcast_fusion), calls=%async_computation.5 | async-start | bytes 1048576 | tf_op jit(solution)/shard_map/all_to_all | solution.py:14

commit v3 on v2

--- a/solution.py
+++ b/solution.py
@@ -38,12 +38,17 @@
     x, core = lax.axis_index("x"), lax.axis_index("core")
     damp_value = damping[0]
 
-    basis = everyones(factor.T, "z")
-    near = everyones(queries, PLANE)
+    own = factor.T
+    other = lax.ppermute(own, "yh", [(0, 1), (1, 0)])
+    near = everyones(queries, "z")
+    other = other + near[:ranks] * 0
+    both = jnp.concatenate([own, other], 0)
+    basis = everyones(both, "x").reshape(-1, width)
 
     mine = lax.dynamic_index_in_dim(
-        eigenvalues.reshape(n_z, -1, ranks), lax.axis_index(("yh", "x")), 1, keepdims=False
-    ).reshape(-1)
+        eigenvalues.reshape(n_z, -1), lax.axis_index("z"), 0, keepdims=False
+    ).reshape(-1, n_x, ranks)
+    mine = jnp.where(lax.axis_index("yh") == 0, mine, mine[::-1]).transpose(1, 0, 2).reshape(-1)
     weights = mine / (mine + damp_value)
 
     partial_value = nt(near, basis).astype(jnp.bfloat16)
@@ -53,7 +58,7 @@
         scaled.astype(jnp.bfloat16), basis, preferred_element_type=jnp.float32
     )
     terms = exchanged(
-        partial_correction.astype(jnp.bfloat16).reshape(-1, rows, width), PLANE
+        partial_correction.astype(jnp.bfloat16).reshape(-1, rows, width), "z"
     )
     correction = terms.astype(jnp.float32).sum(axis=0)
     pre_own = ((queries.astype(jnp.float32) - correction) / damp_value).astype(jnp.bfloat16)

time: 155 us -> 147 us (0.948)
  blocking collectives: 79.6 us -> 41.3 us
  starting transfers between devices: 34 us -> 53 us
  waiting for transfers between devices: 28 us -> 37.8 us
    all_to_all x4 -> x2, blocking collectives: 79.6 us -> 41.3 us  [exchanged(): return lax.all_to_all(tiles, axes, 0, 0, tiled=True)]
    all_to_all x2 -> x4, starting transfers between devices: 15.3 us -> 26.6 us  [exchanged(): return lax.all_to_all(tiles, axes, 0, 0, tiled=True)]
    ppermute x0 -> x1, starting transfers between devices: none -> 7.72 us  [per_device(): other = lax.ppermute(own, 'yh', [(0, 1), (1, 0)])]
    all_to_all x2 -> x4, waiting for transfers between devices: 20.9 us -> 28.2 us  [exchanged(): return lax.all_to_all(tiles, axes, 0, 0, tiled=True)]
    ppermute x0 -> x1, waiting for transfers between devices: none -> 2.88 us  [per_device(): other = lax.ppermute(own, 'yh', [(0, 1), (1, 0)])]
  transfers between devices with their start and end apart: 8 -> 11, of which waited for: 4 -> 7; matrix products, arithmetic and copies ran while one was open for 4% -> 4% of each run, Pallas kernels for 0% -> 0%
where the time goes in v3:
time: 147 us; the launch traced here: 145 us
  starting transfers between devices  53 us (36%)
  blocking collectives  41.3 us (28%)
  waiting for transfers between devices  37.8 us (26%)
  matrix products  6.04 us (4%)
  local copies, waits for them, and re-layouts  4.14 us (3%)
  other arithmetic  2.09 us (1%)
    all_to_all x2, blocking collectives, exchanged(): return lax.all_to_all(tiles, axes, 0, 0, tiled=True)  41.3 us
    all_to_all x4, waiting for transfers between devices, exchanged(): return lax.all_to_all(tiles, axes, 0, 0, tiled=True)  28.2 us
    all_to_all x4, starting transfers between devices, exchanged(): return lax.all_to_all(tiles, axes, 0, 0, tiled=True)  26.6 us
    ppermute x4, starting transfers between devices, from_next(): lax.ppermute(shard, axis, [((i + step) % size, i) for i in range(size)])  14.4 us
    ppermute x1, starting transfers between devices, per_device(): other = lax.ppermute(own, 'yh', [(0, 1), (1, 0)])  7.72 us
    ppermute x4, waiting for transfers between devices, from_next(): lax.ppermute(shard, axis, [((i + step) % size, i) for i in range(size)])  5.98 us
    dot_general x3, matrix products, nt(): lax.dot_general(left, right, (((1,), (1,)), ((), ())), preferred_element_...  5.82 us
    ppermute x2, starting transfers between devices, reduced_on_chip(): came = lax.ppermute(sent.astype(jnp.bfloat16), 'core', [(0, 1), (1, 0)])  4.33 us
  transfers between devices with their start and end apart: 11, of which 7 were waited for; matrix products, arithmetic and copies ran while one was open for 4% of the time, Pallas kernels for 0%

profile of v3, /device:TPU:6, one launch (start us, length us, event | category | flops | bytes accessed | tf_op | source)
XLA Modules:
  0.0 145.3 jit_solution(1503281660728269811)
XLA Ops:
  0.0 0.0 copy-start
  0.0 0.0 copy-start.2
  0.0 1.5 %broadcast_in_dim.8 = bf16[8,8,2048]{2,1,0:T(8,128)(2,1)} broadcast(bf16[8,2048]{1,0:T(8,128)(2,1)} %param.5), dimensions={1,2} | broadcast | bytes 294912 | tf_op jit(solution)/shard_map/broadcast_in_dim | solution.py:19
  1.6 10.3 %all-to-all-start = ((bf16[8,8,2048]{2,1,0:T(8,128)(2,1)}), bf16[8,8,2048]{2,1,0:T(8,128)(2,1)S(1)}, u32[]{:S(2)}, u32[]{:S(2)}) async-start(bf16[8,8,2048]{2,1,0:T(8,128)(2,1)} %broadcast_in_dim.8), calls=%async_computation | async-start | bytes 524288 | tf_op jit(solution)/shard_map/all_to_all | solution.py:14
  11.9 7.7 %collective-permute-start = (bf16[16,2048]{1,0:T(8,128)(2,1)}, bf16[16,2048]{1,0:T(8,128)(2,1)S(1)}, u32[]{:S(2)}, u32[]{:S(2)}) collective-permute-start(bf16[16,2048]{1,0:T(8,128)(2,1)} %bitcast.59), channel_id=1, source_target_pairs={{0,32},{32,0},{1,33},{33,1},{2,34},{34,2},{3,35},{35,3},{4,36},{36... | collective-permute-start | bytes 196616 | tf_op jit(solution)/shard_map/ppermute | solution.py:42
  19.6 2.9 %collective-permute-done = bf16[16,2048]{1,0:T(8,128)(2,1)S(1)} collective-permute-done((bf16[16,2048]{1,0:T(8,128)(2,1)}, bf16[16,2048]{1,0:T(8,128)(2,1)S(1)}, u32[]{:S(2)}, u32[]{:S(2)}) %collective-permute-start) | collective-permute-done | bytes 65568 | tf_op jit(solution)/shard_map/ppermute | solution.py:42
  22.5 1.3 all-to-all-done
  23.8 0.9 pad_maximum_fusion
  24.6 0.8 broadcast_in_dim.9
  25.5 4.8 %all-to-all-start.1 = ((bf16[4,32,2048]{2,1,0:T(8,128)(2,1)}), bf16[4,32,2048]{2,1,0:T(8,128)(2,1)S(1)}, u32[]{:S(2)}, u32[]{:S(2)}) async-start(bf16[4,32,2048]{2,1,0:T(8,128)(2,1)} %broadcast_in_dim.9), calls=%async_computation.1 | async-start | bytes 1048576 | tf_op jit(solution)/shard_map/all_to_all | solution.py:14
  30.2 0.0 copy-done
  30.3 0.1 reshape.71
  30.3 5.9 %all-to-all-done.1 = bf16[4,32,2048]{2,1,0:T(8,128)(2,1)S(1)} async-done(((bf16[4,32,2048]{2,1,0:T(8,128)(2,1)}), bf16[4,32,2048]{2,1,0:T(8,128)(2,1)S(1)}, u32[]{:S(2)}, u32[]{:S(2)}) %all-to-all-start.1) | async-done | bytes 524320 | tf_op jit(solution)/shard_map/all_to_all | solution.py:14
  36.2 0.3 fusion.7
  36.6 0.7 broadcast_in_dim.10
  37.2 4.9 %all-to-all-start.2 = ((bf16[8,1,64,128]{3,2,1,0:T(8,128)(2,1)}), bf16[8,1,64,128]{3,2,1,0:T(8,128)(2,1)S(1)}, u32[]{:S(2)}, u32[]{:S(2)}) async-start(bf16[8,1,64,128]{3,2,1,0:T(8,128)(2,1)} %broadcast_in_dim.10), calls=%async_computation.2 | async-start | bytes 262144 | tf_op jit(solution)/shard_map/all_to_all | solution.py:14
  42.1 0.1 reshape.72
  42.9 6.0 %all-to-all-done.2 = bf16[8,1,64,128]{3,2,1,0:T(8,128)(2,1)S(1)} async-done(((bf16[8,1,64,128]{3,2,1,0:T(8,128)(2,1)}), bf16[8,1,64,128]{3,2,1,0:T(8,128)(2,1)S(1)}, u32[]{:S(2)}, u32[]{:S(2)}) %all-to-all-start.2) | async-done | bytes 131104 | tf_op jit(solution)/shard_map/all_to_all | solution.py:14
  48.9 0.2 fusion
  49.1 17.0 %all_to_all.30 = bf16[8,8,2048]{2,1,0:T(8,128)(2,1)S(1)} all-to-all(bf16[8,8,2048]{2,1,0:T(8,128)(2,1)S(1)} %fusion), channel_id=1, replica_groups=mesh['z'=8,'yh'=2,'x'=4,'yl'=4,'core'=2] {'z'}, dimensions={0} | all-to-all | bytes 524288 | tf_op jit(solution)/shard_map/all_to_all | solution.py:14
  66.2 0.0 copy-done.2
  66.3 24.3 %all_to_all.31 = bf16[16,8,2048]{2,1,0:T(8,128)(2,1)S(1)} all-to-all(bf16[16,8,2048]{2,1,0:T(8,128)(2,1)S(1)} %broadcast_in_dim.11), channel_id=1, replica_groups=mesh['z'=8,'yh'=2,'x'=4,'yl'=4,'core'=2] {'z','yh'}, dimensions={0} | all-to-all | bytes 1048576 | tf_op jit(solution)/shard_map/all_to_all | solution.py:14
  90.5 1.9 %collective-permute-start.1 = (bf16[128,2048]{1,0:T(8,128)(2,1)S(1)}, bf16[128,2048]{1,0:T(8,128)(2,1)S(1)}, u32[]{:S(2)}, u32[]{:S(2)}) collective-permute-start(bf16[128,2048]{1,0:T(8,128)(2,1)S(1)} %bitcast.56), channel_id=1, source_target_pairs={{8,0},{16,8},{24,16},{0,24},{9,1},{17,9},{25,17},{1,25},{10,2},{18... | collective-permute-start | bytes 1572872 | tf_op jit(solution)/shard_map/ppermute | solution.py:25
  92.4 5.1 %collective-permute-start.2 = (bf16[128,2048]{1,0:T(8,128)(2,1)S(1)}, bf16[128,2048]{1,0:T(8,128)(2,1)S(1)}, u32[]{:S(2)}, u32[]{:S(2)}) collective-permute-start(bf16[128,2048]{1,0:T(8,128)(2,1)S(1)} %bitcast.57), channel_id=1, source_target_pairs={{24,0},{0,8},{8,16},{16,24},{25,1},{1,9},{9,17},{17,25},{26,2},{2,... | collective-permute-start | bytes 1572872 | tf_op jit(solution)/shard_map/ppermute | solution.py:25
  97.6 6.0 %collective-permute-done.1 = bf16[128,2048]{1,0:T(8,128)(2,1)S(1)} collective-permute-done((bf16[128,2048]{1,0:T(8,128)(2,1)S(1)}, bf16[128,2048]{1,0:T(8,128)(2,1)S(1)}, u32[]{:S(2)}, u32[]{:S(2)}) %collective-permute-start.1) | collective-permute-done | bytes 524320 | tf_op jit(solution)/shard_map/ppermute | solution.py:25
  103.6 1.9 %collective-permute-start.4 = (bf16[64,2048]{1,0:T(8,128)(2,1)S(1)}, bf16[64,2048]{1,0:T(8,128)(2,1)S(1)}, u32[]{:S(2)}, u32[]{:S(2)}) collective-permute-start(bf16[64,2048]{1,0:T(8,128)(2,1)S(1)} %slice.23), channel_id=1, source_target_pairs={{8,0},{16,8},{24,16},{0,24},{9,1},{17,9},{25,17},{1,25},{10,2},{18... | collective-permute-start | bytes 786440 | tf_op jit(solution)/shard_map/ppermute | solution.py:25
  105.5 0.0 collective-permute-done.2
  105.5 0.0 copy-start.1
  105.5 5.4 %collective-permute-start.5 = (bf16[64,2048]{1,0:T(8,128)(2,1)S(1)}, bf16[64,2048]{1,0:T(8,128)(2,1)S(1)}, u32[]{:S(2)}, u32[]{:S(2)}) collective-permute-start(bf16[64,2048]{1,0:T(8,128)(2,1)S(1)} %slice.24), channel_id=1, source_target_pairs={{24,0},{0,8},{8,16},{16,24},{25,1},{1,9},{9,17},{17,25},{26,2},{2,... | collective-permute-start | bytes 786440 | tf_op jit(solution)/shard_map/ppermute | solution.py:25
  111.0 4.0 %fusion.1 = f32[384,1024]{1,0:T(8,128)S(1)} fusion(bf16[1024,2048]{1,0:T(8,128)(2,1)} %param.9, bf16[128,2048]{1,0:T(8,128)(2,1)S(1)} %collective-permute-done.2, bf16[128,2048]{1,0:T(8,128)(2,1)S(1)} %collective-permute-done.1, bf16[128,2048]{1,0:T(8,128)(2,1)S(1)} %bitcast.58), kind=kOutput, calls=%fused_computation.2 | convolution fusion | flops 1615331328 | bytes 7340032 | tf_op jit(solution)/shard_map/dot_general | solution.py:29
  115.0 0.1 fusion.13
  115.0 1.9 %collective-permute-start.3 = (bf16[3,4,16,1024]{3,2,0,1:T(8,128)(2,1)S(1)}, bf16[3,4,16,1024]{3,2,0,1:T(8,128)(2,1)S(1)}, u32[]{:S(2)}, u32[]{:S(2)}) collective-permute-start(bf16[3,4,16,1024]{3,2,0,1:T(8,128)(2,1)S(1)} %fusion.13), channel_id=1, source_target_pairs={{0,1},{1,0},{2,3},{3,2},{4,5},{5,4},{6,7},{7,6},{8,9},{9,8},{10,11... | collective-permute-start | bytes 1179656 | tf_op jit(solution)/shard_map/ppermute | solution.py:78
  117.0 0.0 collective-permute-done.4
  117.0 0.0 collective-permute-done.5
  117.0 0.0 copy-done.1
  117.0 1.5 %fusion.9 = f32[128,1024]{1,0:T(8,128)S(1)} fusion(bf16[1024,2048]{1,0:T(8,128)(2,1)S(1)} %copy-done.1, bf16[64,2048]{1,0:T(8,128)(2,1)S(1)} %collective-permute-done.5, bf16[64,2048]{1,0:T(8,128)(2,1)S(1)} %collective-permute-done.4), kind=kOutput, calls=%fused_computation.13 | convolution fusion | flops 537919488 | bytes 5242880 | tf_op jit(solution)/shard_map/dot_general | solution.py:29
  118.5 2.4 %collective-permute-start.6 = (bf16[1,4,16,1024]{3,2,0,1:T(8,128)(2,1)S(1)}, bf16[1,4,16,1024]{3,2,0,1:T(8,128)(2,1)S(1)}, u32[]{:S(2)}, u32[]{:S(2)}) collective-permute-start(bf16[1,4,16,1024]{3,2,0,1:T(8,128)(2,1)S(1)} %fusion.16), channel_id=1, source_target_pairs={{0,1},{1,0},{2,3},{3,2},{4,5},{5,4},{6,7},{7,6},{8,9},{9,8},{10,11... | collective-permute-start | bytes 393224 | tf_op jit(solution)/shard_map/ppermute | solution.py:78
  121.0 0.0 collective-permute-done.3
  121.0 0.1 fusion.8
  121.1 0.8 collective-permute-done.6
  122.0 0.9 maximum_bitcast_fusion
  122.8 6.7 %all-to-all-start.5 = ((bf16[4,4,16,1024]{3,2,1,0:T(8,128)(2,1)}), bf16[4,4,16,1024]{3,2,1,0:T(8,128)(2,1)S(1)}, u32[]{:S(2)}, u32[]{:S(2)}) async-start(bf16[4,4,16,1024]{3,2,1,0:T(8,128)(2,1)} %maximum_bitcast_fusion), calls=%async_computation.5 | async-start | bytes 1048576 | tf_op jit(solution)/shard_map/all_to_all | solution.py:14
  129.5 15.0 %all-to-all-done.5 = bf16[4,4,16,1024]{3,2,1,0:T(8,128)(2,1)S(1)} async-done(((bf16[4,4,16,1024]{3,2,1,0:T(8,128)(2,1)}), bf16[4,4,16,1024]{3,2,1,0:T(8,128)(2,1)S(1)}, u32[]{:S(2)}, u32[]{:S(2)}) %all-to-all-start.5) | async-done | bytes 524320 | tf_op jit(solution)/shard_map/all_to_all | solution.py:14
  144.5 0.1 reduce_sum.32
  144.6 0.1 fusion.18
  144.6 0.7 copy.24
  (15 shorter events, 0.3 us)
Async XLA Ops:
  0.0 30.2 %copy-start = (f32[1024]{0:T(1024)S(1)}, f32[1024]{0:T(1024)}, u32[]{:S(2)}) copy-start(f32[1024]{0:T(1024)} %param.7) | copy-start | bytes 12292
  0.0 66.2 %copy-start.2 = (bf16[8,2048]{1,0:T(8,128)(2,1)S(1)}, bf16[8,2048]{1,0:T(8,128)(2,1)}, u32[]{:S(2)}) copy-start(bf16[8,2048]{1,0:T(8,128)(2,1)} %param.5) | copy-start | bytes 98308
  1.6 22.2 %all-to-all-start = ((bf16[8,8,2048]{2,1,0:T(8,128)(2,1)}), bf16[8,8,2048]{2,1,0:T(8,128)(2,1)S(1)}, u32[]{:S(2)}, u32[]{:S(2)}) async-start(bf16[8,8,2048]{2,1,0:T(8,128)(2,1)} %broadcast_in_dim.8), calls=%async_computation | async-start | bytes 524288 | tf_op jit(solution)/shard_map/all_to_all | solution.py:14
  11.9 10.6 %collective-permute-start = (bf16[16,2048]{1,0:T(8,128)(2,1)}, bf16[16,2048]{1,0:T(8,128)(2,1)S(1)}, u32[]{:S(2)}, u32[]{:S(2)}) collective-permute-start(bf16[16,2048]{1,0:T(8,128)(2,1)} %bitcast.59), channel_id=1, source_target_pairs={{0,32},{32,0},{1,33},{33,1},{2,34},{34,2},{3,35},{35,3},{4,36},{36... | collective-permute-start | bytes 196616 | tf_op jit(solution)/shard_map/ppermute | solution.py:42
  25.5 10.8 %all-to-all-start.1 = ((bf16[4,32,2048]{2,1,0:T(8,128)(2,1)}), bf16[4,32,2048]{2,1,0:T(8,128)(2,1)S(1)}, u32[]{:S(2)}, u32[]{:S(2)}) async-start(bf16[4,32,2048]{2,1,0:T(8,128)(2,1)} %broadcast_in_dim.9), calls=%async_computation.1 | async-start | bytes 1048576 | tf_op jit(solution)/shard_map/all_to_all | solution.py:14
  37.2 11.7 %all-to-all-start.2 = ((bf16[8,1,64,128]{3,2,1,0:T(8,128)(2,1)}), bf16[8,1,64,128]{3,2,1,0:T(8,128)(2,1)S(1)}, u32[]{:S(2)}, u32[]{:S(2)}) async-start(bf16[8,1,64,128]{3,2,1,0:T(8,128)(2,1)} %broadcast_in_dim.10), calls=%async_computation.2 | async-start | bytes 262144 | tf_op jit(solution)/shard_map/all_to_all | solution.py:14
  90.5 13.0 %collective-permute-start.1 = (bf16[128,2048]{1,0:T(8,128)(2,1)S(1)}, bf16[128,2048]{1,0:T(8,128)(2,1)S(1)}, u32[]{:S(2)}, u32[]{:S(2)}) collective-permute-start(bf16[128,2048]{1,0:T(8,128)(2,1)S(1)} %bitcast.56), channel_id=1, source_target_pairs={{8,0},{16,8},{24,16},{0,24},{9,1},{17,9},{25,17},{1,25},{10,2},{18... | collective-permute-start | bytes 1572872 | tf_op jit(solution)/shard_map/ppermute | solution.py:25
  92.4 13.1 %collective-permute-start.2 = (bf16[128,2048]{1,0:T(8,128)(2,1)S(1)}, bf16[128,2048]{1,0:T(8,128)(2,1)S(1)}, u32[]{:S(2)}, u32[]{:S(2)}) collective-permute-start(bf16[128,2048]{1,0:T(8,128)(2,1)S(1)} %bitcast.57), channel_id=1, source_target_pairs={{24,0},{0,8},{8,16},{16,24},{25,1},{1,9},{9,17},{17,25},{26,2},{2,... | collective-permute-start | bytes 1572872 | tf_op jit(solution)/shard_map/ppermute | solution.py:25
  103.6 13.4 %collective-permute-start.4 = (bf16[64,2048]{1,0:T(8,128)(2,1)S(1)}, bf16[64,2048]{1,0:T(8,128)(2,1)S(1)}, u32[]{:S(2)}, u32[]{:S(2)}) collective-permute-start(bf16[64,2048]{1,0:T(8,128)(2,1)S(1)} %slice.23), channel_id=1, source_target_pairs={{8,0},{16,8},{24,16},{0,24},{9,1},{17,9},{25,17},{1,25},{10,2},{18... | collective-permute-start | bytes 786440 | tf_op jit(solution)/shard_map/ppermute | solution.py:25
  105.5 11.4 %copy-start.1 = (bf16[1024,2048]{1,0:T(8,128)(2,1)S(1)}, bf16[1024,2048]{1,0:T(8,128)(2,1)}, u32[]{:S(2)}) copy-start(bf16[1024,2048]{1,0:T(8,128)(2,1)} %param.9) | copy-start | bytes 12582916
  105.5 11.4 %collective-permute-start.5 = (bf16[64,2048]{1,0:T(8,128)(2,1)S(1)}, bf16[64,2048]{1,0:T(8,128)(2,1)S(1)}, u32[]{:S(2)}, u32[]{:S(2)}) collective-permute-start(bf16[64,2048]{1,0:T(8,128)(2,1)S(1)} %slice.24), channel_id=1, source_target_pairs={{24,0},{0,8},{8,16},{16,24},{25,1},{1,9},{9,17},{17,25},{26,2},{2,... | collective-permute-start | bytes 786440 | tf_op jit(solution)/shard_map/ppermute | solution.py:25
  115.0 5.9 %collective-permute-start.3 = (bf16[3,4,16,1024]{3,2,0,1:T(8,128)(2,1)S(1)}, bf16[3,4,16,1024]{3,2,0,1:T(8,128)(2,1)S(1)}, u32[]{:S(2)}, u32[]{:S(2)}) collective-permute-start(bf16[3,4,16,1024]{3,2,0,1:T(8,128)(2,1)S(1)} %fusion.13), channel_id=1, source_target_pairs={{0,1},{1,0},{2,3},{3,2},{4,5},{5,4},{6,7},{7,6},{8,9},{9,8},{10,11... | collective-permute-start | bytes 1179656 | tf_op jit(solution)/shard_map/ppermute | solution.py:78
  118.5 3.4 %collective-permute-start.6 = (bf16[1,4,16,1024]{3,2,0,1:T(8,128)(2,1)S(1)}, bf16[1,4,16,1024]{3,2,0,1:T(8,128)(2,1)S(1)}, u32[]{:S(2)}, u32[]{:S(2)}) collective-permute-start(bf16[1,4,16,1024]{3,2,0,1:T(8,128)(2,1)S(1)} %fusion.16), channel_id=1, source_target_pairs={{0,1},{1,0},{2,3},{3,2},{4,5},{5,4},{6,7},{7,6},{8,9},{9,8},{10,11... | collective-permute-start | bytes 393224 | tf_op jit(solution)/shard_map/ppermute | solution.py:78
  122.8 21.7 %all-to-all-start.5 = ((bf16[4,4,16,1024]{3,2,1,0:T(8,128)(2,1)}), bf16[4,4,16,1024]{3,2,1,0:T(8,128)(2,1)S(1)}, u32[]{:S(2)}, u32[]{:S(2)}) async-start(bf16[4,4,16,1024]{3,2,1,0:T(8,128)(2,1)} %maximum_bitcast_fusion), calls=%async_computation.5 | async-start | bytes 1048576 | tf_op jit(solution)/shard_map/all_to_all | solution.py:14

commit v4 on v3

--- a/solution.py
+++ b/solution.py
@@ -1,6 +1,8 @@
 import jax
 import jax.numpy as jnp
 from jax import lax
+from jax.experimental import pallas as pl
+from jax.experimental.pallas import tpu as pltpu
 from jax.sharding import Mesh
 from jax.sharding import PartitionSpec as P
 
@@ -29,6 +31,39 @@
     return lax.dot_general(
         left, right, (((1,), (1,)), ((), ())), preferred_element_type=jnp.float32
     )
+
+
+def chunk_scores(blocks, train_rows, core, run):
+    total = sum(b.shape[0] for b in blocks)
+    groups, (n_train, width) = total // (2 * run), train_rows.shape
+    step = 256
+
+    def kernel(core_ref, *refs):
+        block_refs, (train_ref, kept_ref, sent_ref) = refs[:-3], refs[-3:]
+        left = jnp.concatenate([r[...] for r in block_refs], 0)
+        first = core_ref[0] == 0
+        for start in range(0, n_train, step):
+            value = nt(left, train_ref[start : start + step, :]).reshape(groups, 2, run, step)
+            low, high = value[:, 0], value[:, 1]
+            kept_ref[:, :, start : start + step] = jnp.where(first, low, high)
+            sent_ref[:, :, start : start + step] = jnp.where(first, high, low).astype(jnp.bfloat16)
+
+    vmem = pl.BlockSpec(memory_space=pltpu.VMEM)
+    return pl.pallas_call(
+        kernel,
+        out_shape=(
+            jax.ShapeDtypeStruct((groups, run, n_train), jnp.float32),
+            jax.ShapeDtypeStruct((groups, run, n_train), jnp.bfloat16),
+        ),
+        in_specs=[pl.BlockSpec(memory_space=pltpu.SMEM)] + [vmem] * (len(blocks) + 1),
+        out_specs=(vmem, vmem),
+        compiler_params=pltpu.CompilerParams(vmem_limit_bytes=16 * 1024 * 1024),
+        cost_estimate=pl.CostEstimate(
+            flops=12 * total * n_train * width,
+            bytes_accessed=2 * (total + n_train) * width + 3 * total * n_train,
+            transcendentals=0,
+        ),
+    )(core.reshape(1).astype(jnp.int32), *blocks, train_rows)
 
 
 def per_device(queries, factor, eigenvalues, damping, train_rows):
@@ -64,19 +99,17 @@
     pre_own = ((queries.astype(jnp.float32) - correction) / damp_value).astype(jnp.bfloat16)
 
     chunk = everyones(pre_own, ROWS)
-    half = chunk.shape[0] // 2
+    half = chunk.shape[0] * 5 // 8
     after = from_next(chunk, "x", 1)
     before = from_next(chunk, "x", n_x - 1)
     far_after = from_next(after[:half], "x", 1)
     far_before = from_next(before[half:], "x", n_x - 1)
 
     def reduced_on_chip(blocks):
-        value = nt(jnp.concatenate(blocks, 0), train_rows)
-        value = value.reshape(-1, lax.axis_size("yl"), 2, chunk.shape[0] // n_z, train_rows.shape[0])
-        kept = lax.dynamic_index_in_dim(value, core, 2, keepdims=False)
-        sent = lax.dynamic_index_in_dim(value, 1 - core, 2, keepdims=False)
-        came = lax.ppermute(sent.astype(jnp.bfloat16), "core", [(0, 1), (1, 0)])
-        return (kept + came.astype(jnp.float32)).astype(jnp.bfloat16)
+        kept, sent = chunk_scores(blocks, train_rows, core, chunk.shape[0] // n_z)
+        came = lax.ppermute(sent, "core", [(0, 1), (1, 0)])
+        value = (kept + came.astype(jnp.float32)).astype(jnp.bfloat16)
+        return value.reshape(-1, lax.axis_size("yl"), *value.shape[1:])
 
     first = reduced_on_chip((chunk, after, before))
     last = reduced_on_chip((far_after, far_before))

time: 147 us -> 146 us (level)
  matrix products: 6.04 us -> 0.52 us
  Pallas kernels: 0 us -> 3.31 us
  local copies, waits for them, and re-layouts: 4.14 us -> 6.23 us
    dot_general x3 -> x1, matrix products: 5.82 us -> 0.3 us  [nt(): lax.dot_general(left, right, (((1,), (1,)), ((), ())), preferred_element_...]
    pallas_call x0 -> x2, Pallas kernels: none -> 3.31 us  [chunk_scores(): pl.pallas_call(kernel, out_shape=(jax.ShapeDtypeStruct((groups, run, n_tr...]
    unnamed x6, local copies, waits for them, and re-layouts: 0.01 us -> 2.19 us
  transfers between devices with their start and end apart: 11 -> 11, of which waited for: 7 -> 7; matrix products, arithmetic and copies ran while one was open for 4% -> 0% of each run, Pallas kernels for 0% -> 2%
where the time goes in v4:
time: 146 us; the launch traced here: 145 us
  starting transfers between devices  52.7 us (36%)
  blocking collectives  41.3 us (28%)
  waiting for transfers between devices  37.9 us (26%)
  local copies, waits for them, and re-layouts  6.23 us (4%)
  Pallas kernels  3.31 us (2%)
  other arithmetic  2.05 us (1%)
    all_to_all x2, blocking collectives, exchanged(): return lax.all_to_all(tiles, axes, 0, 0, tiled=True)  41.3 us
    all_to_all x4, waiting for transfers between devices, exchanged(): return lax.all_to_all(tiles, axes, 0, 0, tiled=True)  28.2 us
    all_to_all x4, starting transfers between devices, exchanged(): return lax.all_to_all(tiles, axes, 0, 0, tiled=True)  26.4 us
    ppermute x4, starting transfers between devices, from_next(): lax.ppermute(shard, axis, [((i + step) % size, i) for i in range(size)])  14.3 us
    ppermute x1, starting transfers between devices, per_device(): other = lax.ppermute(own, 'yh', [(0, 1), (1, 0)])  7.72 us
    ppermute x4, waiting for transfers between devices, from_next(): lax.ppermute(shard, axis, [((i + step) % size, i) for i in range(size)])  5.98 us
    ppermute x2, starting transfers between devices, reduced_on_chip(): came = lax.ppermute(sent, 'core', [(0, 1), (1, 0)])  4.33 us
    pallas_call x2, Pallas kernels, chunk_scores(): pl.pallas_call(kernel, out_shape=(jax.ShapeDtypeStruct((groups, run, n_tr...  3.31 us
  transfers between devices with their start and end apart: 11, of which 7 were waited for; matrix products, arithmetic and copies ran while one was open for 0% of the time, Pallas kernels for 2%

profile of v4, /device:TPU:6, one launch (start us, length us, event | category | flops | bytes accessed | tf_op | source)
XLA Modules:
  0.0 144.9 jit_solution(6987332993873386684)
XLA Ops:
  0.0 0.0 copy-start
  0.0 0.0 copy-start.2
  0.0 1.5 %broadcast_in_dim.8 = bf16[8,8,2048]{2,1,0:T(8,128)(2,1)} broadcast(bf16[8,2048]{1,0:T(8,128)(2,1)} %param.5), dimensions={1,2} | broadcast | bytes 294912 | tf_op jit(solution)/shard_map/broadcast_in_dim | solution.py:21
  1.5 10.3 %all-to-all-start = ((bf16[8,8,2048]{2,1,0:T(8,128)(2,1)}), bf16[8,8,2048]{2,1,0:T(8,128)(2,1)S(1)}, u32[]{:S(2)}, u32[]{:S(2)}) async-start(bf16[8,8,2048]{2,1,0:T(8,128)(2,1)} %broadcast_in_dim.8), calls=%async_computation | async-start | bytes 524288 | tf_op jit(solution)/shard_map/all_to_all | solution.py:16
  11.9 7.7 %collective-permute-start = (bf16[16,2048]{1,0:T(8,128)(2,1)}, bf16[16,2048]{1,0:T(8,128)(2,1)S(1)}, u32[]{:S(2)}, u32[]{:S(2)}) collective-permute-start(bf16[16,2048]{1,0:T(8,128)(2,1)} %bitcast.46), channel_id=1, source_target_pairs={{0,32},{32,0},{1,33},{33,1},{2,34},{34,2},{3,35},{35,3},{4,36},{36... | collective-permute-start | bytes 196616 | tf_op jit(solution)/shard_map/ppermute | solution.py:77
  19.6 2.9 %collective-permute-done = bf16[16,2048]{1,0:T(8,128)(2,1)S(1)} collective-permute-done((bf16[16,2048]{1,0:T(8,128)(2,1)}, bf16[16,2048]{1,0:T(8,128)(2,1)S(1)}, u32[]{:S(2)}, u32[]{:S(2)}) %collective-permute-start) | collective-permute-done | bytes 65568 | tf_op jit(solution)/shard_map/ppermute | solution.py:77
  22.5 1.3 all-to-all-done
  23.8 0.9 pad_maximum_fusion
  24.6 0.9 broadcast_in_dim.9
  25.5 4.8 %all-to-all-start.1 = ((bf16[4,32,2048]{2,1,0:T(8,128)(2,1)}), bf16[4,32,2048]{2,1,0:T(8,128)(2,1)S(1)}, u32[]{:S(2)}, u32[]{:S(2)}) async-start(bf16[4,32,2048]{2,1,0:T(8,128)(2,1)} %broadcast_in_dim.9), calls=%async_computation.1 | async-start | bytes 1048576 | tf_op jit(solution)/shard_map/all_to_all | solution.py:16
  30.2 0.0 copy-done
  30.3 0.1 reshape.62
  30.3 5.9 %all-to-all-done.1 = bf16[4,32,2048]{2,1,0:T(8,128)(2,1)S(1)} async-done(((bf16[4,32,2048]{2,1,0:T(8,128)(2,1)}), bf16[4,32,2048]{2,1,0:T(8,128)(2,1)S(1)}, u32[]{:S(2)}, u32[]{:S(2)}) %all-to-all-start.1) | async-done | bytes 524320 | tf_op jit(solution)/shard_map/all_to_all | solution.py:16
  36.2 0.3 fusion.1
  36.6 0.7 broadcast_in_dim.10
  37.2 4.9 %all-to-all-start.2 = ((bf16[8,1,64,128]{3,2,1,0:T(8,128)(2,1)}), bf16[8,1,64,128]{3,2,1,0:T(8,128)(2,1)S(1)}, u32[]{:S(2)}, u32[]{:S(2)}) async-start(bf16[8,1,64,128]{3,2,1,0:T(8,128)(2,1)} %broadcast_in_dim.10), calls=%async_computation.2 | async-start | bytes 262144 | tf_op jit(solution)/shard_map/all_to_all | solution.py:16
  42.1 0.1 reshape.63
  42.9 6.0 %all-to-all-done.2 = bf16[8,1,64,128]{3,2,1,0:T(8,128)(2,1)S(1)} async-done(((bf16[8,1,64,128]{3,2,1,0:T(8,128)(2,1)}), bf16[8,1,64,128]{3,2,1,0:T(8,128)(2,1)S(1)}, u32[]{:S(2)}, u32[]{:S(2)}) %all-to-all-start.2) | async-done | bytes 131104 | tf_op jit(solution)/shard_map/all_to_all | solution.py:16
  48.9 0.2 fusion
  49.1 17.0 %all_to_all.30 = bf16[8,8,2048]{2,1,0:T(8,128)(2,1)S(1)} all-to-all(bf16[8,8,2048]{2,1,0:T(8,128)(2,1)S(1)} %fusion), channel_id=1, replica_groups=mesh['z'=8,'yh'=2,'x'=4,'yl'=4,'core'=2] {'z'}, dimensions={0} | all-to-all | bytes 524288 | tf_op jit(solution)/shard_map/all_to_all | solution.py:16
  66.2 0.0 copy-done.2
  66.2 24.3 %all_to_all.31 = bf16[16,8,2048]{2,1,0:T(8,128)(2,1)S(1)} all-to-all(bf16[16,8,2048]{2,1,0:T(8,128)(2,1)S(1)} %broadcast_in_dim.11), channel_id=1, replica_groups=mesh['z'=8,'yh'=2,'x'=4,'yl'=4,'core'=2] {'z','yh'}, dimensions={0} | all-to-all | bytes 1048576 | tf_op jit(solution)/shard_map/all_to_all | solution.py:16
  90.5 1.9 %collective-permute-start.1 = (bf16[128,2048]{1,0:T(8,128)(2,1)S(1)}, bf16[128,2048]{1,0:T(8,128)(2,1)S(1)}, u32[]{:S(2)}, u32[]{:S(2)}) collective-permute-start(bf16[128,2048]{1,0:T(8,128)(2,1)S(1)} %bitcast.40), channel_id=1, source_target_pairs={{8,0},{16,8},{24,16},{0,24},{9,1},{17,9},{25,17},{1,25},{10,2},{18... | collective-permute-start | bytes 1572872 | tf_op jit(solution)/shard_map/ppermute | solution.py:27
  92.4 5.1 %collective-permute-start.2 = (bf16[128,2048]{1,0:T(8,128)(2,1)S(1)}, bf16[128,2048]{1,0:T(8,128)(2,1)S(1)}, u32[]{:S(2)}, u32[]{:S(2)}) collective-permute-start(bf16[128,2048]{1,0:T(8,128)(2,1)S(1)} %bitcast.41), channel_id=1, source_target_pairs={{24,0},{0,8},{8,16},{16,24},{25,1},{1,9},{9,17},{17,25},{26,2},{2,... | collective-permute-start | bytes 1572872 | tf_op jit(solution)/shard_map/ppermute | solution.py:27
  97.6 6.0 %collective-permute-done.1.refs_1_ = bf16[128,2048]{1,0:T(8,128)(2,1)S(1)} collective-permute-done((bf16[128,2048]{1,0:T(8,128)(2,1)S(1)}, bf16[128,2048]{1,0:T(8,128)(2,1)S(1)}, u32[]{:S(2)}, u32[]{:S(2)}) %collective-permute-start.1) | collective-permute-done | bytes 524320 | tf_op jit(solution)/shard_map/ppermute | solution.py:27
  103.6 1.9 %collective-permute-start.4 = (bf16[80,2048]{1,0:T(8,128)(2,1)S(1)}, bf16[80,2048]{1,0:T(8,128)(2,1)S(1)}, u32[]{:S(2)}, u32[]{:S(2)}) collective-permute-start(bf16[80,2048]{1,0:T(8,128)(2,1)S(1)} %slice.31), channel_id=1, source_target_pairs={{8,0},{16,8},{24,16},{0,24},{9,1},{17,9},{25,17},{1,25},{10,2},{18... | collective-permute-start | bytes 983048 | tf_op jit(solution)/shard_map/ppermute | solution.py:27
  105.5 0.0 collective-permute-done.2.refs_2_
  105.5 5.3 %collective-permute-start.5 = (bf16[48,2048]{1,0:T(8,128)(2,1)S(1)}, bf16[48,2048]{1,0:T(8,128)(2,1)S(1)}, u32[]{:S(2)}, u32[]{:S(2)}) collective-permute-start(bf16[48,2048]{1,0:T(8,128)(2,1)S(1)} %slice.32), channel_id=1, source_target_pairs={{24,0},{0,8},{8,16},{16,24},{25,1},{1,9},{9,17},{17,25},{26,2},{2,... | collective-permute-start | bytes 589832 | tf_op jit(solution)/shard_map/ppermute | solution.py:27
  110.9 0.0 copy-start.1
  110.9 2.2 %copy-done.1 = bf16[1024,2048]{1,0:T(8,128)(2,1)S(1)} copy-done((bf16[1024,2048]{1,0:T(8,128)(2,1)S(1)}, bf16[1024,2048]{1,0:T(8,128)(2,1)}, u32[]{:S(2)}) %copy-start.1) | copy-done | bytes 4194328
  113.1 1.8 %shard_map.55 = (f32[12,16,1024]{2,1,0:T(8,128)S(1)}, bf16[12,16,1024]{2,1,0:T(8,128)(2,1)S(1)}) custom-call(s32[1]{0:T(128)} %bitcast.core_ref, bf16[128,2048]{1,0:T(8,128)(2,1)S(1)} %bitcast.42, bf16[128,2048]{1,0:T(8,128)(2,1)S(1)} %collective-permute-done.1.refs_1_, bf16[128,2048]{1,0:T(8,128)(2,1)S(1)} %collective-permute-done.2.refs_2_, ...), custom_call_target="tpu_custom_call" | custom-call | flops 9663676416 | bytes 6946816 | tf_op jit(solution)/shard_map/pallas_call | solution.py:52
  114.9 1.9 %collective-permute-start.3 = (bf16[12,16,1024]{2,1,0:T(8,128)(2,1)S(1)}, bf16[12,16,1024]{2,1,0:T(8,128)(2,1)S(1)}, u32[]{:S(2)}, u32[]{:S(2)}) collective-permute-start(bf16[12,16,1024]{2,1,0:T(8,128)(2,1)S(1)} %get-tuple-element.10), channel_id=1, source_target_pairs={{0,1},{1,0},{2,3},{3,2},{4,5},{5,4},{6,7},{7,6},{8,9},{9,8},{10,11... | collective-permute-start | bytes 1179656 | tf_op jit(solution)/shard_map/ppermute | solution.py:110
  116.8 0.0 collective-permute-done.5.refs_1_
  116.8 0.0 collective-permute-done.4.refs_0_
  116.8 1.5 %shard_map.56 = (f32[4,16,1024]{2,1,0:T(8,128)S(1)}, bf16[4,16,1024]{2,1,0:T(8,128)(2,1)S(1)}) custom-call(s32[1]{0:T(128)} %bitcast.core_ref, bf16[80,2048]{1,0:T(8,128)(2,1)S(1)} %collective-permute-done.4.refs_0_, bf16[48,2048]{1,0:T(8,128)(2,1)S(1)} %collective-permute-done.5.refs_1_, bf16[1024,2048]{1,0:T(8,128)(2,1)S(1)} %copy-done.1), custom_call_target="tpu_custom_call" | custom-call | flops 3221225472 | bytes 5111808 | tf_op jit(solution)/shard_map/pallas_call | solution.py:52
  118.3 2.4 %collective-permute-start.6 = (bf16[4,16,1024]{2,1,0:T(8,128)(2,1)S(1)}, bf16[4,16,1024]{2,1,0:T(8,128)(2,1)S(1)}, u32[]{:S(2)}, u32[]{:S(2)}) collective-permute-start(bf16[4,16,1024]{2,1,0:T(8,128)(2,1)S(1)} %get-tuple-element.12), channel_id=1, source_target_pairs={{0,1},{1,0},{2,3},{3,2},{4,5},{5,4},{6,7},{7,6},{8,9},{9,8},{10,11... | collective-permute-start | bytes 393224 | tf_op jit(solution)/shard_map/ppermute | solution.py:110
  120.8 0.0 collective-permute-done.3
  120.8 0.1 add_convert_fusion
  120.9 0.8 collective-permute-done.6
  121.8 0.8 maximum_bitcast_fusion
  122.6 6.4 %all-to-all-start.5 = ((bf16[4,4,16,1024]{3,2,1,0:T(8,128)(2,1)}), bf16[4,4,16,1024]{3,2,1,0:T(8,128)(2,1)S(1)}, u32[]{:S(2)}, u32[]{:S(2)}) async-start(bf16[4,4,16,1024]{3,2,1,0:T(8,128)(2,1)} %maximum_bitcast_fusion), calls=%async_computation.5 | async-start | bytes 1048576 | tf_op jit(solution)/shard_map/all_to_all | solution.py:16
  129.0 15.0 %all-to-all-done.5 = bf16[4,4,16,1024]{3,2,1,0:T(8,128)(2,1)S(1)} async-done(((bf16[4,4,16,1024]{3,2,1,0:T(8,128)(2,1)}), bf16[4,4,16,1024]{3,2,1,0:T(8,128)(2,1)S(1)}, u32[]{:S(2)}, u32[]{:S(2)}) %all-to-all-start.5) | async-done | bytes 524320 | tf_op jit(solution)/shard_map/all_to_all | solution.py:16
  144.0 0.1 reduce_sum.32
  144.1 0.1 fusion.5
  144.2 0.7 copy.21
  (14 shorter events, 0.3 us)
Async XLA Ops:
  0.0 30.2 %copy-start = (f32[1024]{0:T(1024)S(1)}, f32[1024]{0:T(1024)}, u32[]{:S(2)}) copy-start(f32[1024]{0:T(1024)} %param.7) | copy-start | bytes 12292
  0.0 66.2 %copy-start.2 = (bf16[8,2048]{1,0:T(8,128)(2,1)S(1)}, bf16[8,2048]{1,0:T(8,128)(2,1)}, u32[]{:S(2)}) copy-start(bf16[8,2048]{1,0:T(8,128)(2,1)} %param.5) | copy-start | bytes 98308
  1.5 22.2 %all-to-all-start = ((bf16[8,8,2048]{2,1,0:T(8,128)(2,1)}), bf16[8,8,2048]{2,1,0:T(8,128)(2,1)S(1)}, u32[]{:S(2)}, u32[]{:S(2)}) async-start(bf16[8,8,2048]{2,1,0:T(8,128)(2,1)} %broadcast_in_dim.8), calls=%async_computation | async-start | bytes 524288 | tf_op jit(solution)/shard_map/all_to_all | solution.py:16
  11.9 10.6 %collective-permute-start = (bf16[16,2048]{1,0:T(8,128)(2,1)}, bf16[16,2048]{1,0:T(8,128)(2,1)S(1)}, u32[]{:S(2)}, u32[]{:S(2)}) collective-permute-start(bf16[16,2048]{1,0:T(8,128)(2,1)} %bitcast.46), channel_id=1, source_target_pairs={{0,32},{32,0},{1,33},{33,1},{2,34},{34,2},{3,35},{35,3},{4,36},{36... | collective-permute-start | bytes 196616 | tf_op jit(solution)/shard_map/ppermute | solution.py:77
  25.5 10.8 %all-to-all-start.1 = ((bf16[4,32,2048]{2,1,0:T(8,128)(2,1)}), bf16[4,32,2048]{2,1,0:T(8,128)(2,1)S(1)}, u32[]{:S(2)}, u32[]{:S(2)}) async-start(bf16[4,32,2048]{2,1,0:T(8,128)(2,1)} %broadcast_in_dim.9), calls=%async_computation.1 | async-start | bytes 1048576 | tf_op jit(solution)/shard_map/all_to_all | solution.py:16
  37.2 11.7 %all-to-all-start.2 = ((bf16[8,1,64,128]{3,2,1,0:T(8,128)(2,1)}), bf16[8,1,64,128]{3,2,1,0:T(8,128)(2,1)S(1)}, u32[]{:S(2)}, u32[]{:S(2)}) async-start(bf16[8,1,64,128]{3,2,1,0:T(8,128)(2,1)} %broadcast_in_dim.10), calls=%async_computation.2 | async-start | bytes 262144 | tf_op jit(solution)/shard_map/all_to_all | solution.py:16
  90.5 13.0 %collective-permute-start.1 = (bf16[128,2048]{1,0:T(8,128)(2,1)S(1)}, bf16[128,2048]{1,0:T(8,128)(2,1)S(1)}, u32[]{:S(2)}, u32[]{:S(2)}) collective-permute-start(bf16[128,2048]{1,0:T(8,128)(2,1)S(1)} %bitcast.40), channel_id=1, source_target_pairs={{8,0},{16,8},{24,16},{0,24},{9,1},{17,9},{25,17},{1,25},{10,2},{18... | collective-permute-start | bytes 1572872 | tf_op jit(solution)/shard_map/ppermute | solution.py:27
  92.4 13.1 %collective-permute-start.2 = (bf16[128,2048]{1,0:T(8,128)(2,1)S(1)}, bf16[128,2048]{1,0:T(8,128)(2,1)S(1)}, u32[]{:S(2)}, u32[]{:S(2)}) collective-permute-start(bf16[128,2048]{1,0:T(8,128)(2,1)S(1)} %bitcast.41), channel_id=1, source_target_pairs={{24,0},{0,8},{8,16},{16,24},{25,1},{1,9},{9,17},{17,25},{26,2},{2,... | collective-permute-start | bytes 1572872 | tf_op jit(solution)/shard_map/ppermute | solution.py:27
  103.6 13.3 %collective-permute-start.4 = (bf16[80,2048]{1,0:T(8,128)(2,1)S(1)}, bf16[80,2048]{1,0:T(8,128)(2,1)S(1)}, u32[]{:S(2)}, u32[]{:S(2)}) collective-permute-start(bf16[80,2048]{1,0:T(8,128)(2,1)S(1)} %slice.31), channel_id=1, source_target_pairs={{8,0},{16,8},{24,16},{0,24},{9,1},{17,9},{25,17},{1,25},{10,2},{18... | collective-permute-start | bytes 983048 | tf_op jit(solution)/shard_map/ppermute | solution.py:27
  105.5 11.3 %collective-permute-start.5 = (bf16[48,2048]{1,0:T(8,128)(2,1)S(1)}, bf16[48,2048]{1,0:T(8,128)(2,1)S(1)}, u32[]{:S(2)}, u32[]{:S(2)}) collective-permute-start(bf16[48,2048]{1,0:T(8,128)(2,1)S(1)} %slice.32), channel_id=1, source_target_pairs={{24,0},{0,8},{8,16},{16,24},{25,1},{1,9},{9,17},{17,25},{26,2},{2,... | collective-permute-start | bytes 589832 | tf_op jit(solution)/shard_map/ppermute | solution.py:27
  110.9 2.2 %copy-start.1 = (bf16[1024,2048]{1,0:T(8,128)(2,1)S(1)}, bf16[1024,2048]{1,0:T(8,128)(2,1)}, u32[]{:S(2)}) copy-start(bf16[1024,2048]{1,0:T(8,128)(2,1)} %refs_2_.1) | copy-start | bytes 12582916
  114.9 5.9 %collective-permute-start.3 = (bf16[12,16,1024]{2,1,0:T(8,128)(2,1)S(1)}, bf16[12,16,1024]{2,1,0:T(8,128)(2,1)S(1)}, u32[]{:S(2)}, u32[]{:S(2)}) collective-permute-start(bf16[12,16,1024]{2,1,0:T(8,128)(2,1)S(1)} %get-tuple-element.10), channel_id=1, source_target_pairs={{0,1},{1,0},{2,3},{3,2},{4,5},{5,4},{6,7},{7,6},{8,9},{9,8},{10,11... | collective-permute-start | bytes 1179656 | tf_op jit(solution)/shard_map/ppermute | solution.py:110
  118.3 3.4 %collective-permute-start.6 = (bf16[4,16,1024]{2,1,0:T(8,128)(2,1)S(1)}, bf16[4,16,1024]{2,1,0:T(8,128)(2,1)S(1)}, u32[]{:S(2)}, u32[]{:S(2)}) collective-permute-start(bf16[4,16,1024]{2,1,0:T(8,128)(2,1)S(1)} %get-tuple-element.12), channel_id=1, source_target_pairs={{0,1},{1,0},{2,3},{3,2},{4,5},{5,4},{6,7},{7,6},{8,9},{9,8},{10,11... | collective-permute-start | bytes 393224 | tf_op jit(solution)/shard_map/ppermute | solution.py:110
  122.6 21.4 %all-to-all-start.5 = ((bf16[4,4,16,1024]{3,2,1,0:T(8,128)(2,1)}), bf16[4,4,16,1024]{3,2,1,0:T(8,128)(2,1)S(1)}, u32[]{:S(2)}, u32[]{:S(2)}) async-start(bf16[4,4,16,1024]{3,2,1,0:T(8,128)(2,1)} %maximum_bitcast_fusion), calls=%async_computation.5 | async-start | bytes 1048576 | tf_op jit(solution)/shard_map/all_to_all | solution.py:16

commit v5 on v4

--- a/solution.py
+++ b/solution.py
@@ -66,6 +66,23 @@
     )(core.reshape(1).astype(jnp.int32), *blocks, train_rows)
 
 
+def repeated_pair(top, bottom, copies, after):
+    def kernel(top_ref, bottom_ref, _, out_ref):
+        both = jnp.concatenate([top_ref[...], bottom_ref[...]], 0)
+        for i in range(copies):
+            out_ref[i] = both
+
+    vmem = pl.BlockSpec(memory_space=pltpu.VMEM)
+    shape = (copies, top.shape[0] + bottom.shape[0], top.shape[1])
+    return pl.pallas_call(
+        kernel,
+        out_shape=jax.ShapeDtypeStruct(shape, top.dtype),
+        in_specs=[vmem, vmem, pl.BlockSpec(memory_space=pl.ANY)],
+        out_specs=vmem,
+        compiler_params=pltpu.CompilerParams(vmem_limit_bytes=12 * 1024 * 1024),
+    )(top, bottom, after)
+
+
 def per_device(queries, factor, eigenvalues, damping, train_rows):
     rows, width = queries.shape
     ranks = factor.shape[1]
@@ -76,9 +93,8 @@
     own = factor.T
     other = lax.ppermute(own, "yh", [(0, 1), (1, 0)])
     near = everyones(queries, "z")
-    other = other + near[:ranks] * 0
-    both = jnp.concatenate([own, other], 0)
-    basis = everyones(both, "x").reshape(-1, width)
+    held = own + queries[:1] * 0
+    basis = exchanged(repeated_pair(held, other, n_x, near), "x").reshape(-1, width)
 
     mine = lax.dynamic_index_in_dim(
         eigenvalues.reshape(n_z, -1), lax.axis_index("z"), 0, keepdims=False

time: 146 us -> 145 us (level)
  blocking collectives: 41.3 us -> 35.2 us
  waiting for transfers between devices: 37.9 us -> 43.4 us
    all_to_all x4, waiting for transfers between devices: 28.2 us -> 36.8 us  [exchanged(): return lax.all_to_all(tiles, axes, 0, 0, tiled=True)]
    all_to_all x2, blocking collectives: 41.3 us -> 35.2 us  [exchanged(): return lax.all_to_all(tiles, axes, 0, 0, tiled=True)]
    ppermute x1, waiting for transfers between devices: 2.88 us -> 0.01 us  [per_device(): other = lax.ppermute(own, 'yh', [(0, 1), (1, 0)])]
    broadcast_in_dim x4 -> x3, local copies, waits for them, and re-layouts: 3.12 us -> 2.19 us  [everyones(): tiles = exchanged(jnp.broadcast_to(shard[None], (size, *shard.shape)), axes)]
  transfers between devices with their start and end apart: 11 -> 11, of which waited for: 7 -> 6; matrix products, arithmetic and copies ran while one was open for 0% -> 2% of each run, Pallas kernels for 2% -> 2%
where the time goes in v5:
time: 145 us; the launch traced here: 144 us
  starting transfers between devices  51.6 us (36%)
  waiting for transfers between devices  43.4 us (30%)
  blocking collectives  35.2 us (24%)
  local copies, waits for them, and re-layouts  5.31 us (4%)
  Pallas kernels  4.12 us (3%)
  other arithmetic  2.82 us (2%)
    all_to_all x4, waiting for transfers between devices, exchanged(): return lax.all_to_all(tiles, axes, 0, 0, tiled=True)  36.8 us
    all_to_all x2, blocking collectives, exchanged(): return lax.all_to_all(tiles, axes, 0, 0, tiled=True)  35.2 us
    all_to_all x4, starting transfers between devices, exchanged(): return lax.all_to_all(tiles, axes, 0, 0, tiled=True)  25.1 us
    ppermute x4, starting transfers between devices, from_next(): lax.ppermute(shard, axis, [((i + step) % size, i) for i in range(size)])  14.3 us
    ppermute x1, starting transfers between devices, per_device(): other = lax.ppermute(own, 'yh', [(0, 1), (1, 0)])  7.85 us
    ppermute x4, waiting for transfers between devices, from_next(): lax.ppermute(shard, axis, [((i + step) % size, i) for i in range(size)])  5.83 us
    ppermute x2, starting transfers between devices, reduced_on_chip(): came = lax.ppermute(sent, 'core', [(0, 1), (1, 0)])  4.33 us
    pallas_call x2, Pallas kernels, chunk_scores(): pl.pallas_call(kernel, out_shape=(jax.ShapeDtypeStruct((groups, run, n_tr...  3.3 us
  transfers between devices with their start and end apart: 11, of which 6 were waited for; matrix products, arithmetic and copies ran while one was open for 2% of the time, Pallas kernels for 2%

profile of v5, /device:TPU:6, one launch (start us, length us, event | category | flops | bytes accessed | tf_op | source)
XLA Modules:
  0.0 143.9 jit_solution(15166609349275583142)
XLA Ops:
  0.0 0.0 copy-start
  0.0 0.0 copy-start.2
  0.0 7.9 %collective-permute-start = (bf16[16,2048]{1,0:T(8,128)(2,1)}, bf16[16,2048]{1,0:T(8,128)(2,1)S(1)}, u32[]{:S(2)}, u32[]{:S(2)}) collective-permute-start(bf16[16,2048]{1,0:T(8,128)(2,1)} %bitcast.44), channel_id=1, source_target_pairs={{0,32},{32,0},{1,33},{33,1},{2,34},{34,2},{3,35},{35,3},{4,36},{36... | collective-permute-start | bytes 196616 | tf_op jit(solution)/shard_map/ppermute | solution.py:94
  7.9 1.5 %broadcast_in_dim.6 = bf16[8,8,2048]{2,1,0:T(8,128)(2,1)} broadcast(bf16[8,2048]{1,0:T(8,128)(2,1)} %param.5), dimensions={1,2} | broadcast | bytes 294912 | tf_op jit(solution)/shard_map/broadcast_in_dim | solution.py:21
  9.3 10.3 %all-to-all-start = ((bf16[8,8,2048]{2,1,0:T(8,128)(2,1)}), bf16[8,8,2048]{2,1,0:T(8,128)(2,1)S(1)}, u32[]{:S(2)}, u32[]{:S(2)}) async-start(bf16[8,8,2048]{2,1,0:T(8,128)(2,1)} %broadcast_in_dim.6), calls=%async_computation | async-start | bytes 524288 | tf_op jit(solution)/shard_map/all_to_all | solution.py:16
  19.7 0.8 multiply_reduce_fusion
  20.4 0.9 broadcast_add_fusion.top_ref
  21.3 0.0 collective-permute-done.bottom_ref
  21.3 9.9 %all-to-all-done = bf16[8,8,2048]{2,1,0:T(8,128)(2,1)S(1)} async-done(((bf16[8,8,2048]{2,1,0:T(8,128)(2,1)}), bf16[8,8,2048]{2,1,0:T(8,128)(2,1)S(1)}, u32[]{:S(2)}, u32[]{:S(2)}) %all-to-all-start) | async-done | bytes 262176 | tf_op jit(solution)/shard_map/all_to_all | solution.py:16
  31.3 0.8 shard_map.55
  32.1 4.8 %all-to-all-start.1 = ((bf16[4,32,2048]{2,1,0:T(8,128)(2,1)}), bf16[4,32,2048]{2,1,0:T(8,128)(2,1)S(1)}, u32[]{:S(2)}, u32[]{:S(2)}) async-start(bf16[4,32,2048]{2,1,0:T(8,128)(2,1)} %shard_map.55), calls=%async_computation.1 | async-start | bytes 1048576 | tf_op jit(solution)/shard_map/all_to_all | solution.py:16
  36.8 0.0 copy-done
  36.9 0.1 reshape.58
  37.0 5.9 %all-to-all-done.1 = bf16[4,32,2048]{2,1,0:T(8,128)(2,1)S(1)} async-done(((bf16[4,32,2048]{2,1,0:T(8,128)(2,1)}), bf16[4,32,2048]{2,1,0:T(8,128)(2,1)S(1)}, u32[]{:S(2)}, u32[]{:S(2)}) %all-to-all-start.1) | async-done | bytes 524320 | tf_op jit(solution)/shard_map/all_to_all | solution.py:16
  42.9 0.3 fusion.1
  43.2 0.7 broadcast_in_dim.7
  43.8 3.4 %all-to-all-start.2 = ((bf16[8,1,64,128]{3,2,1,0:T(8,128)(2,1)}), bf16[8,1,64,128]{3,2,1,0:T(8,128)(2,1)S(1)}, u32[]{:S(2)}, u32[]{:S(2)}) async-start(bf16[8,1,64,128]{3,2,1,0:T(8,128)(2,1)} %broadcast_in_dim.7), calls=%async_computation.2 | async-start | bytes 262144 | tf_op jit(solution)/shard_map/all_to_all | solution.py:16
  47.2 0.1 reshape.59
  48.0 5.9 %all-to-all-done.2 = bf16[8,1,64,128]{3,2,1,0:T(8,128)(2,1)S(1)} async-done(((bf16[8,1,64,128]{3,2,1,0:T(8,128)(2,1)}), bf16[8,1,64,128]{3,2,1,0:T(8,128)(2,1)S(1)}, u32[]{:S(2)}, u32[]{:S(2)}) %all-to-all-start.2) | async-done | bytes 131104 | tf_op jit(solution)/shard_map/all_to_all | solution.py:16
  54.0 0.2 fusion
  54.2 14.3 %all_to_all.30 = bf16[8,8,2048]{2,1,0:T(8,128)(2,1)S(1)} all-to-all(bf16[8,8,2048]{2,1,0:T(8,128)(2,1)S(1)} %fusion), channel_id=1, replica_groups=mesh['z'=8,'yh'=2,'x'=4,'yl'=4,'core'=2] {'z'}, dimensions={0} | all-to-all | bytes 524288 | tf_op jit(solution)/shard_map/all_to_all | solution.py:16
  68.5 0.0 copy-done.2
  68.6 20.9 %all_to_all.31 = bf16[16,8,2048]{2,1,0:T(8,128)(2,1)S(1)} all-to-all(bf16[16,8,2048]{2,1,0:T(8,128)(2,1)S(1)} %broadcast_in_dim.8), channel_id=1, replica_groups=mesh['z'=8,'yh'=2,'x'=4,'yl'=4,'core'=2] {'z','yh'}, dimensions={0} | all-to-all | bytes 1048576 | tf_op jit(solution)/shard_map/all_to_all | solution.py:16
  89.5 1.9 %collective-permute-start.1 = (bf16[128,2048]{1,0:T(8,128)(2,1)S(1)}, bf16[128,2048]{1,0:T(8,128)(2,1)S(1)}, u32[]{:S(2)}, u32[]{:S(2)}) collective-permute-start(bf16[128,2048]{1,0:T(8,128)(2,1)S(1)} %bitcast.38), channel_id=1, source_target_pairs={{8,0},{16,8},{24,16},{0,24},{9,1},{17,9},{25,17},{1,25},{10,2},{18... | collective-permute-start | bytes 1572872 | tf_op jit(solution)/shard_map/ppermute | solution.py:27
  91.4 5.1 %collective-permute-start.2 = (bf16[128,2048]{1,0:T(8,128)(2,1)S(1)}, bf16[128,2048]{1,0:T(8,128)(2,1)S(1)}, u32[]{:S(2)}, u32[]{:S(2)}) collective-permute-start(bf16[128,2048]{1,0:T(8,128)(2,1)S(1)} %bitcast.39), channel_id=1, source_target_pairs={{24,0},{0,8},{8,16},{16,24},{25,1},{1,9},{9,17},{17,25},{26,2},{2,... | collective-permute-start | bytes 1572872 | tf_op jit(solution)/shard_map/ppermute | solution.py:27
  96.6 5.8 %collective-permute-done.1.refs_1_ = bf16[128,2048]{1,0:T(8,128)(2,1)S(1)} collective-permute-done((bf16[128,2048]{1,0:T(8,128)(2,1)S(1)}, bf16[128,2048]{1,0:T(8,128)(2,1)S(1)}, u32[]{:S(2)}, u32[]{:S(2)}) %collective-permute-start.1) | collective-permute-done | bytes 524320 | tf_op jit(solution)/shard_map/ppermute | solution.py:27
  102.4 1.9 %collective-permute-start.4 = (bf16[80,2048]{1,0:T(8,128)(2,1)S(1)}, bf16[80,2048]{1,0:T(8,128)(2,1)S(1)}, u32[]{:S(2)}, u32[]{:S(2)}) collective-permute-start(bf16[80,2048]{1,0:T(8,128)(2,1)S(1)} %slice.29), channel_id=1, source_target_pairs={{8,0},{16,8},{24,16},{0,24},{9,1},{17,9},{25,17},{1,25},{10,2},{18... | collective-permute-start | bytes 983048 | tf_op jit(solution)/shard_map/ppermute | solution.py:27
  104.3 0.0 collective-permute-done.2.refs_2_
  104.4 5.3 %collective-permute-start.5 = (bf16[48,2048]{1,0:T(8,128)(2,1)S(1)}, bf16[48,2048]{1,0:T(8,128)(2,1)S(1)}, u32[]{:S(2)}, u32[]{:S(2)}) collective-permute-start(bf16[48,2048]{1,0:T(8,128)(2,1)S(1)} %slice.30), channel_id=1, source_target_pairs={{24,0},{0,8},{8,16},{16,24},{25,1},{1,9},{9,17},{17,25},{26,2},{2,... | collective-permute-start | bytes 589832 | tf_op jit(solution)/shard_map/ppermute | solution.py:27
  109.7 0.0 copy-start.1
  109.7 2.2 %copy-done.1 = bf16[1024,2048]{1,0:T(8,128)(2,1)S(1)} copy-done((bf16[1024,2048]{1,0:T(8,128)(2,1)S(1)}, bf16[1024,2048]{1,0:T(8,128)(2,1)}, u32[]{:S(2)}) %copy-start.1) | copy-done | bytes 4194328
  111.9 1.8 %shard_map.56 = (f32[12,16,1024]{2,1,0:T(8,128)S(1)}, bf16[12,16,1024]{2,1,0:T(8,128)(2,1)S(1)}) custom-call(s32[1]{0:T(128)} %bitcast.core_ref, bf16[128,2048]{1,0:T(8,128)(2,1)S(1)} %bitcast.40, bf16[128,2048]{1,0:T(8,128)(2,1)S(1)} %collective-permute-done.1.refs_1_, bf16[128,2048]{1,0:T(8,128)(2,1)S(1)} %collective-permute-done.2.refs_2_, ...), custom_call_target="tpu_custom_call" | custom-call | flops 9663676416 | bytes 6946816 | tf_op jit(solution)/shard_map/pallas_call | solution.py:52
  113.7 1.9 %collective-permute-start.3 = (bf16[12,16,1024]{2,1,0:T(8,128)(2,1)S(1)}, bf16[12,16,1024]{2,1,0:T(8,128)(2,1)S(1)}, u32[]{:S(2)}, u32[]{:S(2)}) collective-permute-start(bf16[12,16,1024]{2,1,0:T(8,128)(2,1)S(1)} %get-tuple-element.10), channel_id=1, source_target_pairs={{0,1},{1,0},{2,3},{3,2},{4,5},{5,4},{6,7},{7,6},{8,9},{9,8},{10,11... | collective-permute-start | bytes 1179656 | tf_op jit(solution)/shard_map/ppermute | solution.py:126
  115.7 0.0 collective-permute-done.5.refs_1_
  115.7 0.0 collective-permute-done.4.refs_0_
  115.7 1.5 %shard_map.57 = (f32[4,16,1024]{2,1,0:T(8,128)S(1)}, bf16[4,16,1024]{2,1,0:T(8,128)(2,1)S(1)}) custom-call(s32[1]{0:T(128)} %bitcast.core_ref, bf16[80,2048]{1,0:T(8,128)(2,1)S(1)} %collective-permute-done.4.refs_0_, bf16[48,2048]{1,0:T(8,128)(2,1)S(1)} %collective-permute-done.5.refs_1_, bf16[1024,2048]{1,0:T(8,128)(2,1)S(1)} %copy-done.1), custom_call_target="tpu_custom_call" | custom-call | flops 3221225472 | bytes 5111808 | tf_op jit(solution)/shard_map/pallas_call | solution.py:52
  117.2 2.4 %collective-permute-start.6 = (bf16[4,16,1024]{2,1,0:T(8,128)(2,1)S(1)}, bf16[4,16,1024]{2,1,0:T(8,128)(2,1)S(1)}, u32[]{:S(2)}, u32[]{:S(2)}) collective-permute-start(bf16[4,16,1024]{2,1,0:T(8,128)(2,1)S(1)} %get-tuple-element.12), channel_id=1, source_target_pairs={{0,1},{1,0},{2,3},{3,2},{4,5},{5,4},{6,7},{7,6},{8,9},{9,8},{10,11... | collective-permute-start | bytes 393224 | tf_op jit(solution)/shard_map/ppermute | solution.py:126
  119.6 0.0 collective-permute-done.3
  119.6 0.1 add_convert_fusion
  119.7 0.8 collective-permute-done.6
  120.6 0.8 maximum_bitcast_fusion
  121.4 6.6 %all-to-all-start.5 = ((bf16[4,4,16,1024]{3,2,1,0:T(8,128)(2,1)}), bf16[4,4,16,1024]{3,2,1,0:T(8,128)(2,1)S(1)}, u32[]{:S(2)}, u32[]{:S(2)}) async-start(bf16[4,4,16,1024]{3,2,1,0:T(8,128)(2,1)} %maximum_bitcast_fusion), calls=%async_computation.5 | async-start | bytes 1048576 | tf_op jit(solution)/shard_map/all_to_all | solution.py:16
  128.0 15.0 %all-to-all-done.5 = bf16[4,4,16,1024]{3,2,1,0:T(8,128)(2,1)S(1)} async-done(((bf16[4,4,16,1024]{3,2,1,0:T(8,128)(2,1)}), bf16[4,4,16,1024]{3,2,1,0:T(8,128)(2,1)S(1)}, u32[]{:S(2)}, u32[]{:S(2)}) %all-to-all-start.5) | async-done | bytes 524320 | tf_op jit(solution)/shard_map/all_to_all | solution.py:16
  143.0 0.1 reduce_sum.32
  143.1 0.1 fusion.4
  143.2 0.7 copy.21
  (13 shorter events, 0.2 us)
Async XLA Ops:
  0.0 36.8 %copy-start = (f32[1024]{0:T(1024)S(1)}, f32[1024]{0:T(1024)}, u32[]{:S(2)}) copy-start(f32[1024]{0:T(1024)} %param.7) | copy-start | bytes 12292
  0.0 68.5 %copy-start.2 = (bf16[8,2048]{1,0:T(8,128)(2,1)S(1)}, bf16[8,2048]{1,0:T(8,128)(2,1)}, u32[]{:S(2)}) copy-start(bf16[8,2048]{1,0:T(8,128)(2,1)} %param.5) | copy-start | bytes 98308
  0.0 21.3 %collective-permute-start = (bf16[16,2048]{1,0:T(8,128)(2,1)}, bf16[16,2048]{1,0:T(8,128)(2,1)S(1)}, u32[]{:S(2)}, u32[]{:S(2)}) collective-permute-start(bf16[16,2048]{1,0:T(8,128)(2,1)} %bitcast.44), channel_id=1, source_target_pairs={{0,32},{32,0},{1,33},{33,1},{2,34},{34,2},{3,35},{35,3},{4,36},{36... | collective-permute-start | bytes 196616 | tf_op jit(solution)/shard_map/ppermute | solution.py:94
  9.3 21.9 %all-to-all-start = ((bf16[8,8,2048]{2,1,0:T(8,128)(2,1)}), bf16[8,8,2048]{2,1,0:T(8,128)(2,1)S(1)}, u32[]{:S(2)}, u32[]{:S(2)}) async-start(bf16[8,8,2048]{2,1,0:T(8,128)(2,1)} %broadcast_in_dim.6), calls=%async_computation | async-start | bytes 524288 | tf_op jit(solution)/shard_map/all_to_all | solution.py:16
  32.1 10.8 %all-to-all-start.1 = ((bf16[4,32,2048]{2,1,0:T(8,128)(2,1)}), bf16[4,32,2048]{2,1,0:T(8,128)(2,1)S(1)}, u32[]{:S(2)}, u32[]{:S(2)}) async-start(bf16[4,32,2048]{2,1,0:T(8,128)(2,1)} %shard_map.55), calls=%async_computation.1 | async-start | bytes 1048576 | tf_op jit(solution)/shard_map/all_to_all | solution.py:16
  43.8 10.1 %all-to-all-start.2 = ((bf16[8,1,64,128]{3,2,1,0:T(8,128)(2,1)}), bf16[8,1,64,128]{3,2,1,0:T(8,128)(2,1)S(1)}, u32[]{:S(2)}, u32[]{:S(2)}) async-start(bf16[8,1,64,128]{3,2,1,0:T(8,128)(2,1)} %broadcast_in_dim.7), calls=%async_computation.2 | async-start | bytes 262144 | tf_op jit(solution)/shard_map/all_to_all | solution.py:16
  89.5 12.9 %collective-permute-start.1 = (bf16[128,2048]{1,0:T(8,128)(2,1)S(1)}, bf16[128,2048]{1,0:T(8,128)(2,1)S(1)}, u32[]{:S(2)}, u32[]{:S(2)}) collective-permute-start(bf16[128,2048]{1,0:T(8,128)(2,1)S(1)} %bitcast.38), channel_id=1, source_target_pairs={{8,0},{16,8},{24,16},{0,24},{9,1},{17,9},{25,17},{1,25},{10,2},{18... | collective-permute-start | bytes 1572872 | tf_op jit(solution)/shard_map/ppermute | solution.py:27
  91.4 12.9 %collective-permute-start.2 = (bf16[128,2048]{1,0:T(8,128)(2,1)S(1)}, bf16[128,2048]{1,0:T(8,128)(2,1)S(1)}, u32[]{:S(2)}, u32[]{:S(2)}) collective-permute-start(bf16[128,2048]{1,0:T(8,128)(2,1)S(1)} %bitcast.39), channel_id=1, source_target_pairs={{24,0},{0,8},{8,16},{16,24},{25,1},{1,9},{9,17},{17,25},{26,2},{2,... | collective-permute-start | bytes 1572872 | tf_op jit(solution)/shard_map/ppermute | solution.py:27
  102.4 13.3 %collective-permute-start.4 = (bf16[80,2048]{1,0:T(8,128)(2,1)S(1)}, bf16[80,2048]{1,0:T(8,128)(2,1)S(1)}, u32[]{:S(2)}, u32[]{:S(2)}) collective-permute-start(bf16[80,2048]{1,0:T(8,128)(2,1)S(1)} %slice.29), channel_id=1, source_target_pairs={{8,0},{16,8},{24,16},{0,24},{9,1},{17,9},{25,17},{1,25},{10,2},{18... | collective-permute-start | bytes 983048 | tf_op jit(solution)/shard_map/ppermute | solution.py:27
  104.4 11.3 %collective-permute-start.5 = (bf16[48,2048]{1,0:T(8,128)(2,1)S(1)}, bf16[48,2048]{1,0:T(8,128)(2,1)S(1)}, u32[]{:S(2)}, u32[]{:S(2)}) collective-permute-start(bf16[48,2048]{1,0:T(8,128)(2,1)S(1)} %slice.30), channel_id=1, source_target_pairs={{24,0},{0,8},{8,16},{16,24},{25,1},{1,9},{9,17},{17,25},{26,2},{2,... | collective-permute-start | bytes 589832 | tf_op jit(solution)/shard_map/ppermute | solution.py:27
  109.7 2.2 %copy-start.1 = (bf16[1024,2048]{1,0:T(8,128)(2,1)S(1)}, bf16[1024,2048]{1,0:T(8,128)(2,1)}, u32[]{:S(2)}) copy-start(bf16[1024,2048]{1,0:T(8,128)(2,1)} %refs_2_.1) | copy-start | bytes 12582916
  113.7 5.9 %collective-permute-start.3 = (bf16[12,16,1024]{2,1,0:T(8,128)(2,1)S(1)}, bf16[12,16,1024]{2,1,0:T(8,128)(2,1)S(1)}, u32[]{:S(2)}, u32[]{:S(2)}) collective-permute-start(bf16[12,16,1024]{2,1,0:T(8,128)(2,1)S(1)} %get-tuple-element.10), channel_id=1, source_target_pairs={{0,1},{1,0},{2,3},{3,2},{4,5},{5,4},{6,7},{7,6},{8,9},{9,8},{10,11... | collective-permute-start | bytes 1179656 | tf_op jit(solution)/shard_map/ppermute | solution.py:126
  117.2 3.4 %collective-permute-start.6 = (bf16[4,16,1024]{2,1,0:T(8,128)(2,1)S(1)}, bf16[4,16,1024]{2,1,0:T(8,128)(2,1)S(1)}, u32[]{:S(2)}, u32[]{:S(2)}) collective-permute-start(bf16[4,16,1024]{2,1,0:T(8,128)(2,1)S(1)} %get-tuple-element.12), channel_id=1, source_target_pairs={{0,1},{1,0},{2,3},{3,2},{4,5},{5,4},{6,7},{7,6},{8,9},{9,8},{10,11... | collective-permute-start | bytes 393224 | tf_op jit(solution)/shard_map/ppermute | solution.py:126
  121.4 21.6 %all-to-all-start.5 = ((bf16[4,4,16,1024]{3,2,1,0:T(8,128)(2,1)}), bf16[4,4,16,1024]{3,2,1,0:T(8,128)(2,1)S(1)}, u32[]{:S(2)}, u32[]{:S(2)}) async-start(bf16[4,4,16,1024]{3,2,1,0:T(8,128)(2,1)} %maximum_bitcast_fusion), calls=%async_computation.5 | async-start | bytes 1048576 | tf_op jit(solution)/shard_map/all_to_all | solution.py:16
